TPU v7x, 256 devices: a whole 4x4x8 slice. The times are simulated.
256 devices in a mesh: phase: 2 (over x_hi), bank: 16 (over x_lo, y, core), blk: 8 (over z).
Axes of the slice: x: 4 (x_hi: 2, x_lo: 2; x = x_hi * 2 + x_lo), y: 4, z: 8, core: 2. Of those that a mesh axis runs over, the one named last changes fastest.
Arguments:
- query_clips: bfloat16 [16, 1024, 128], P('blk', 'bank'), may hold values from -6 to 6
- conv_weight: bfloat16 [4, 3, 1024, 32], P('phase', None, 'bank'), may hold values from -0.625 to 0.625
- mix_weight: bfloat16 [4, 1024, 1024], P('phase', 'bank'), may hold values from -0.1875 to 0.1875
- proj_weight: bfloat16 [512, 1024], P(None, 'bank'), may hold values from -0.25 to 0.25
- taps: float32 [7], replicated, may hold values from 0.25 to 1
- reference_frames: bfloat16 [524288, 512], P(('phase', 'bank', 'blk')), may hold values from -6 to 6
- slice_lengths: int32 [256, 16], P(('phase', 'bank', 'blk')), may hold values from 1 to 256, 2048 in all within a row
Outputs:
- tile_maxima: float32 [16, 4096], P(None, ('phase', 'bank', 'blk'))
Inputs may be any that keep to these rules, and one draw needn't show every extreme that they name: `slice_lengths`: each row sums to 2048, and the largest entry of every row is 256.
All inputs are finite; a program needn't handle non-finite values.
Results may differ from a plain program's by a relative error of at most 0.004.
Values may be sent and summed in bfloat16 or wider, within the bound.
A program may use at most 64 MiB of HBM per device.

v0:
```python
import jax
import jax.numpy as jnp
from jax import lax
from jax.sharding import PartitionSpec as P

TILE = 128
TAPS = 7


def from_behind(value, axis, by):
    devices = lax.axis_size(axis)
    pairs = [(i, i + by) for i in range(devices) if 0 <= i + by < devices]
    return lax.ppermute(value, axis, pairs)


def broadcast(block, axis, owner):
    block = jnp.where(lax.axis_index(axis) == owner, block, jnp.zeros_like(block))
    return lax.psum(block, axis)


def shifted(block, axis, distance):
    devices = range(lax.axis_size(axis))
    route = [((i - distance) % len(devices), i) for i in devices]
    return lax.ppermute(block, axis, route)


def encode_layer(hidden_state, conv_local, mix_local, dilation, pad_reach, total_channels):
    clip_count, channels, frames = hidden_state.shape
    group_width = conv_local.shape[2]
    groups = channels // group_width
    padded = jnp.pad(hidden_state, ((0, 0), (0, 0), (pad_reach, pad_reach)))
    summed = jnp.zeros((clip_count, groups, group_width, frames), jnp.float32)
    for tap_index in range(3):
        window = lax.dynamic_slice_in_dim(padded, pad_reach + (tap_index - 1) * dilation, frames, 2)
        window = window.reshape(clip_count, groups, group_width, frames)
        kernel = conv_local[tap_index].reshape(groups, group_width, group_width)
        summed = summed + jnp.einsum(
            "bgit,goi->bgot", window, kernel, preferred_element_type=jnp.float32
        )
    activated = (
        jax.nn.gelu(summed, approximate=True)
        .astype(jnp.bfloat16)
        .reshape(clip_count, channels, frames)
    )
    piece_rows = lax.all_gather(activated, "bank", axis=1, tiled=True)
    mixed_sum = jnp.einsum("oc,bct->bot", mix_local, piece_rows, preferred_element_type=jnp.float32)
    widened = piece_rows.astype(jnp.float32)
    mixed_sum, squares = (mixed_sum, jnp.sum(widened * widened, axis=1))
    mixed_sum = mixed_sum * lax.rsqrt(squares / total_channels + 1e-06)[:, None, :]
    return (hidden_state.astype(jnp.float32) + mixed_sum).astype(jnp.bfloat16)


def per_device(
    query_clips, conv_weight, mix_weight, proj_weight, taps, reference_frames, slice_lengths
):
    phase_index = lax.axis_index("phase")
    phase_count = lax.axis_size("phase")
    per_phase = conv_weight.shape[0]
    layer_total = per_phase * phase_count
    pad_reach = 2 ** (layer_total - 1)
    total_channels = mix_weight.shape[2]
    clip_count = query_clips.shape[0]

    def encode(hidden_state):
        for layer_index in range(per_phase):
            dilation = jnp.left_shift(jnp.int32(1), phase_index * per_phase + layer_index)
            hidden_state = encode_layer(
                hidden_state,
                conv_weight[layer_index],
                mix_weight[layer_index],
                dilation,
                pad_reach,
                total_channels,
            )
        return hidden_state

    first_pass = encode(query_clips)
    received = from_behind(first_pass, "phase", 1)
    encoded = encode(jnp.where(phase_index == 0, jnp.zeros_like(received), received))
    projected = jnp.einsum("ec,bct->bet", proj_weight, encoded, preferred_element_type=jnp.float32)
    features = projected.shape[1]
    summed_all = lax.psum(projected, "bank")
    norm_sums = jnp.sum(summed_all * summed_all, axis=1) / features
    described = (summed_all * lax.rsqrt(norm_sums + 1e-06)[:, None, :]).astype(jnp.bfloat16)
    described = broadcast(described, "phase", 1)
    frame_count = reference_frames.shape[0]
    tile_count = frame_count // TILE
    slice_ends = jnp.cumsum(slice_lengths[0])
    position = jnp.arange(frame_count, dtype=jnp.int32)
    segment = jnp.sum((position[:, None] >= slice_ends[None, :]).astype(jnp.int32), axis=1)
    segment_pad = jnp.pad(segment, (3, 3), constant_values=-1)
    same_slice = [
        segment_pad[shift_index : shift_index + frame_count] == segment
        for shift_index in range(TAPS)
    ]
    factor = features ** (-0.5)

    def score(panel_now):
        rows = panel_now.shape[0]
        frames_per_clip = panel_now.shape[2]
        scores = (
            jnp.einsum(
                "bet,re->btr", panel_now, reference_frames, preferred_element_type=jnp.float32
            )
            * factor
        )
        padded = jnp.pad(scores, ((0, 0), (3, 3), (3, 3)))
        filtered = jnp.zeros_like(scores)
        for shift_index in range(TAPS):
            moved = padded[
                :,
                shift_index : shift_index + frames_per_clip,
                shift_index : shift_index + frame_count,
            ]
            filtered = filtered + taps[shift_index] * jnp.where(
                same_slice[shift_index][None, None, :], moved, 0.0
            )
        return jnp.max(filtered.reshape(rows, frames_per_clip, tile_count, TILE), axis=(1, 3))

    def place(maxima_all, block_maxima, owner_index):
        return lax.dynamic_update_slice_in_dim(
            maxima_all, block_maxima, owner_index * clip_count, 0
        )

    loop_size = lax.axis_size("blk")
    blk_index = lax.axis_index("blk")
    empty = jnp.zeros((clip_count * loop_size, tile_count), jnp.float32)

    def advance(step_index, running):
        panel_now, maxima_all = running
        panel_now = shifted(panel_now, "blk", 1)
        owner_index = (blk_index - step_index) % loop_size
        return (panel_now, place(maxima_all, score(panel_now), owner_index))

    start_state = (described, place(empty, score(described), blk_index))
    panel_now, maxima_all = lax.fori_loop(1, loop_size, advance, start_state)
    return maxima_all


def solution(mesh):
    in_specs = (
        P("blk", "bank", None),
        P("phase", None, "bank", None),
        P("phase", "bank", None),
        P(None, "bank"),
        P(),
        P(("phase", "bank", "blk"), None),
        P(("phase", "bank", "blk"), None),
    )
    out_specs = P(None, ("phase", "bank", "blk"))
    return jax.shard_map(
        per_device, mesh=mesh, in_specs=in_specs, out_specs=out_specs, check_vma=False
    )
```

profile of v0, /device:TPU:1, one launch (start us, length us, event | category | flops | bytes accessed | tf_op | source)
XLA Modules:
  0.0 392.6 jit_solution(5952368467624948342)
XLA Ops:
  6.6 0.8 fusion.126
  7.7 0.9 pad_dynamic-slice_fusion.6
  8.7 0.9 convolution_bitcast_fusion.3
  9.8 22.6 %all_gather.12 = bf16[2,1024,128]{2,1,0:T(8,128)(2,1)S(1)} all-gather(bf16[2,64,128]{2,1,0:T(8,128)(2,1)S(1)} %bitcast.207), channel_id=1, replica_groups=mesh['phase'=2,'bank'=16,'blk'=8] {'bank'}, dimensions={1}, use_global_device_ids=true | all-gather | bytes 557056 | tf_op jit(solution)/shard_map/all_gather | solution.py:45
  33.7 17.7 %all_gather.13 = bf16[2,1024,128]{2,1,0:T(8,128)(2,1)S(1)} all-gather(bf16[2,64,128]{2,1,0:T(8,128)(2,1)S(1)} %bitcast.208), channel_id=1, replica_groups=mesh['phase'=2,'bank'=16,'blk'=8] {'bank'}, dimensions={1}, use_global_device_ids=true | all-gather | bytes 557056 | tf_op jit(solution)/shard_map/all_gather | solution.py:45
  51.8 4.4 %collective-permute-start.1 = (bf16[2,64,128]{2,1,0:T(8,128)(2,1)S(1)}, bf16[2,64,128]{2,1,0:T(8,128)(2,1)S(1)}, u32[]{:S(2)}, u32[]{:S(2)}) collective-permute-start(bf16[2,64,128]{2,1,0:T(8,128)(2,1)S(1)} %fusion.54), channel_id=1, source_target_pairs={{0,128},{1,129},{2,130},{3,131},{4,132},{5,133},{6,134},{7,135},{8... | collective-permute-start | bytes 98312 | tf_op jit(solution)/shard_map/ppermute | solution.py:13
  56.2 1.0 collective-permute-done.1
  57.7 19.9 %all_gather.14 = bf16[2,1024,128]{2,1,0:T(8,128)(2,1)S(1)} all-gather(bf16[2,64,128]{2,1,0:T(8,128)(2,1)S(1)} %bitcast.209), channel_id=1, replica_groups=mesh['phase'=2,'bank'=16,'blk'=8] {'bank'}, dimensions={1}, use_global_device_ids=true | all-gather | bytes 557056 | tf_op jit(solution)/shard_map/all_gather | solution.py:45
  78.5 17.7 %all_gather.15 = bf16[2,1024,128]{2,1,0:T(8,128)(2,1)S(1)} all-gather(bf16[2,64,128]{2,1,0:T(8,128)(2,1)S(1)} %bitcast.210), channel_id=1, replica_groups=mesh['phase'=2,'bank'=16,'blk'=8] {'bank'}, dimensions={1}, use_global_device_ids=true | all-gather | bytes 557056 | tf_op jit(solution)/shard_map/all_gather | solution.py:45
  96.4 1.4 convolution_bitcast_fusion
  98.2 124.2 %all-reduce.10.cloned.1.call-done = f32[2,512,128]{1,2,0:T(8,128)} async-done(((f32[2,512,128]{1,2,0:T(8,128)}), f32[2,512,128]{1,2,0:T(8,128)}) %all-reduce.10.cloned.1.call-update) | async-done | bytes 524304 | tf_op jit(solution)/shard_map/psum | solution.py:82
  222.4 1.2 multiply_reduce_fusion.4
  223.6 1.9 fusion.55
  226.9 35.9 %all-reduce.12.cloned.1.call-done = bf16[2,512,128]{1,2,0:T(8,128)(2,1)} async-done(((bf16[2,512,128]{1,2,0:T(8,128)(2,1)}), bf16[2,512,128]{1,2,0:T(8,128)(2,1)}) %all-reduce.12.cloned.1.call-update) | async-done | bytes 262160 | tf_op jit(solution)/shard_map/psum | solution.py:18
  262.7 1.7 broadcast_multiply_fusion.1
  264.5 8.2 %fusion.41 = f32[2,2048]{1,0:T(2,128)S(1)} fusion(f32[2,128,2048]{2,1,0:T(8,128)S(1)} %get-tuple-element.419, f32[2,128,2048]{2,1,0:T(8,128)S(1)} %get-tuple-element.420, f32[]{:T(128)} %bitcast.77, f32[]{:T(128)} %bitcast.76, f32[]{:T(128)} %bitcast.75, f32[]{:T(128)} %bitcast.74, f32[]{:T(128)} %bitcast.73, f32[]{:T(128)} %bitcast.72, f32[]{:T(128)} %bitcast.69, ...), kind=kLoop, calls=%fused_computation.56 | loop fusion | flops 10481664 | bytes 4223004 | tf_op jit(solution)/shard_map/reduce_max | solution.py:118
  272.8 112.3 %while.18 = (s32[]{:T(128)}, bf16[2,512,128]{1,2,0:T(8,128)(2,1)S(1)}, f32[16,16]{1,0:T(8,128)S(1)}, f32[7]{0:T(128)S(1)}, pred[2048]{0:T(1024)(128)(4,1)S(1)}, ...) while((s32[]{:T(128)}, ...), condition=%wide.region_14.15_spmd, body=%wide.region_11.14_spmd.sunk | while | flops 547880960 | bytes 12368460 | solution.py:136
  272.8 1.4 collective-permute-start
  274.8 6.6 %collective-permute-done = bf16[2,512,128]{1,2,0:T(8,128)(2,1)S(1)} collective-permute-done((bf16[2,512,128]{1,2,0:T(8,128)(2,1)S(1)}, bf16[2,512,128]{1,2,0:T(8,128)(2,1)S(1)}, u32[]{:S(2)}, u32[]{:S(2)}) %collective-permute-start) | collective-permute-done | bytes 262176 | tf_op jit(solution)/shard_map/while/body/eval_jaxpr/ppermute | solution.py:24
  282.2 8.2 %fusion.151 = f32[2,2048]{1,0:T(2,128)S(1)} fusion(f32[2,128,2048]{2,1,0:T(8,128)S(1)} %get-tuple-element.508, f32[2,128,2048]{2,1,0:T(8,128)S(1)} %get-tuple-element.509, f32[]{:T(128)} %bitcast.184, f32[]{:T(128)} %bitcast.185, f32[]{:T(128)} %bitcast.186, f32[]{:T(128)} %get-tuple-element.562, f32[]{:T(128)} %bitcast.187, f32[]{:T(128)} %bitcast.188, ...), kind=kLoop, calls=%fused_computation.26.clone.1 | loop fusion | flops 10481664 | bytes 4223004 | tf_op jit(solution)/shard_map/while/body/eval_jaxpr/reduce_max | solution.py:118
  291.3 6.6 %collective-permute-done = bf16[2,512,128]{1,2,0:T(8,128)(2,1)S(1)} collective-permute-done((bf16[2,512,128]{1,2,0:T(8,128)(2,1)S(1)}, bf16[2,512,128]{1,2,0:T(8,128)(2,1)S(1)}, u32[]{:S(2)}, u32[]{:S(2)}) %collective-permute-start) | collective-permute-done | bytes 262176 | tf_op jit(solution)/shard_map/while/body/eval_jaxpr/ppermute | solution.py:24
  298.7 8.2 %fusion.151 = f32[2,2048]{1,0:T(2,128)S(1)} fusion(f32[2,128,2048]{2,1,0:T(8,128)S(1)} %get-tuple-element.508, f32[2,128,2048]{2,1,0:T(8,128)S(1)} %get-tuple-element.509, f32[]{:T(128)} %bitcast.184, f32[]{:T(128)} %bitcast.185, f32[]{:T(128)} %bitcast.186, f32[]{:T(128)} %get-tuple-element.562, f32[]{:T(128)} %bitcast.187, f32[]{:T(128)} %bitcast.188, ...), kind=kLoop, calls=%fused_computation.26.clone.1 | loop fusion | flops 10481664 | bytes 4223004 | tf_op jit(solution)/shard_map/while/body/eval_jaxpr/reduce_max | solution.py:118
  307.8 5.7 %collective-permute-done = bf16[2,512,128]{1,2,0:T(8,128)(2,1)S(1)} collective-permute-done((bf16[2,512,128]{1,2,0:T(8,128)(2,1)S(1)}, bf16[2,512,128]{1,2,0:T(8,128)(2,1)S(1)}, u32[]{:S(2)}, u32[]{:S(2)}) %collective-permute-start) | collective-permute-done | bytes 262176 | tf_op jit(solution)/shard_map/while/body/eval_jaxpr/ppermute | solution.py:24
  314.3 8.2 %fusion.151 = f32[2,2048]{1,0:T(2,128)S(1)} fusion(f32[2,128,2048]{2,1,0:T(8,128)S(1)} %get-tuple-element.508, f32[2,128,2048]{2,1,0:T(8,128)S(1)} %get-tuple-element.509, f32[]{:T(128)} %bitcast.184, f32[]{:T(128)} %bitcast.185, f32[]{:T(128)} %bitcast.186, f32[]{:T(128)} %get-tuple-element.562, f32[]{:T(128)} %bitcast.187, f32[]{:T(128)} %bitcast.188, ...), kind=kLoop, calls=%fused_computation.26.clone.1 | loop fusion | flops 10481664 | bytes 4223004 | tf_op jit(solution)/shard_map/while/body/eval_jaxpr/reduce_max | solution.py:118
  323.4 5.7 %collective-permute-done = bf16[2,512,128]{1,2,0:T(8,128)(2,1)S(1)} collective-permute-done((bf16[2,512,128]{1,2,0:T(8,128)(2,1)S(1)}, bf16[2,512,128]{1,2,0:T(8,128)(2,1)S(1)}, u32[]{:S(2)}, u32[]{:S(2)}) %collective-permute-start) | collective-permute-done | bytes 262176 | tf_op jit(solution)/shard_map/while/body/eval_jaxpr/ppermute | solution.py:24
  329.9 8.2 %fusion.151 = f32[2,2048]{1,0:T(2,128)S(1)} fusion(f32[2,128,2048]{2,1,0:T(8,128)S(1)} %get-tuple-element.508, f32[2,128,2048]{2,1,0:T(8,128)S(1)} %get-tuple-element.509, f32[]{:T(128)} %bitcast.184, f32[]{:T(128)} %bitcast.185, f32[]{:T(128)} %bitcast.186, f32[]{:T(128)} %get-tuple-element.562, f32[]{:T(128)} %bitcast.187, f32[]{:T(128)} %bitcast.188, ...), kind=kLoop, calls=%fused_computation.26.clone.1 | loop fusion | flops 10481664 | bytes 4223004 | tf_op jit(solution)/shard_map/while/body/eval_jaxpr/reduce_max | solution.py:118
  339.0 5.7 %collective-permute-done = bf16[2,512,128]{1,2,0:T(8,128)(2,1)S(1)} collective-permute-done((bf16[2,512,128]{1,2,0:T(8,128)(2,1)S(1)}, bf16[2,512,128]{1,2,0:T(8,128)(2,1)S(1)}, u32[]{:S(2)}, u32[]{:S(2)}) %collective-permute-start) | collective-permute-done | bytes 262176 | tf_op jit(solution)/shard_map/while/body/eval_jaxpr/ppermute | solution.py:24
  345.6 8.2 %fusion.151 = f32[2,2048]{1,0:T(2,128)S(1)} fusion(f32[2,128,2048]{2,1,0:T(8,128)S(1)} %get-tuple-element.508, f32[2,128,2048]{2,1,0:T(8,128)S(1)} %get-tuple-element.509, f32[]{:T(128)} %bitcast.184, f32[]{:T(128)} %bitcast.185, f32[]{:T(128)} %bitcast.186, f32[]{:T(128)} %get-tuple-element.562, f32[]{:T(128)} %bitcast.187, f32[]{:T(128)} %bitcast.188, ...), kind=kLoop, calls=%fused_computation.26.clone.1 | loop fusion | flops 10481664 | bytes 4223004 | tf_op jit(solution)/shard_map/while/body/eval_jaxpr/reduce_max | solution.py:118
  354.6 5.7 %collective-permute-done = bf16[2,512,128]{1,2,0:T(8,128)(2,1)S(1)} collective-permute-done((bf16[2,512,128]{1,2,0:T(8,128)(2,1)S(1)}, bf16[2,512,128]{1,2,0:T(8,128)(2,1)S(1)}, u32[]{:S(2)}, u32[]{:S(2)}) %collective-permute-start) | collective-permute-done | bytes 262176 | tf_op jit(solution)/shard_map/while/body/eval_jaxpr/ppermute | solution.py:24
  361.2 8.2 %fusion.151 = f32[2,2048]{1,0:T(2,128)S(1)} fusion(f32[2,128,2048]{2,1,0:T(8,128)S(1)} %get-tuple-element.508, f32[2,128,2048]{2,1,0:T(8,128)S(1)} %get-tuple-element.509, f32[]{:T(128)} %bitcast.184, f32[]{:T(128)} %bitcast.185, f32[]{:T(128)} %bitcast.186, f32[]{:T(128)} %get-tuple-element.562, f32[]{:T(128)} %bitcast.187, f32[]{:T(128)} %bitcast.188, ...), kind=kLoop, calls=%fused_computation.26.clone.1 | loop fusion | flops 10481664 | bytes 4223004 | tf_op jit(solution)/shard_map/while/body/eval_jaxpr/reduce_max | solution.py:118
  370.3 5.7 %collective-permute-done = bf16[2,512,128]{1,2,0:T(8,128)(2,1)S(1)} collective-permute-done((bf16[2,512,128]{1,2,0:T(8,128)(2,1)S(1)}, bf16[2,512,128]{1,2,0:T(8,128)(2,1)S(1)}, u32[]{:S(2)}, u32[]{:S(2)}) %collective-permute-start) | collective-permute-done | bytes 262176 | tf_op jit(solution)/shard_map/while/body/eval_jaxpr/ppermute | solution.py:24
  376.8 8.2 %fusion.151 = f32[2,2048]{1,0:T(2,128)S(1)} fusion(f32[2,128,2048]{2,1,0:T(8,128)S(1)} %get-tuple-element.508, f32[2,128,2048]{2,1,0:T(8,128)S(1)} %get-tuple-element.509, f32[]{:T(128)} %bitcast.184, f32[]{:T(128)} %bitcast.185, f32[]{:T(128)} %bitcast.186, f32[]{:T(128)} %get-tuple-element.562, f32[]{:T(128)} %bitcast.187, f32[]{:T(128)} %bitcast.188, ...), kind=kLoop, calls=%fused_computation.26.clone.1 | loop fusion | flops 10481664 | bytes 4223004 | tf_op jit(solution)/shard_map/while/body/eval_jaxpr/reduce_max | solution.py:118
  (107 shorter events, 17.0 us)
Async XLA Ops:
  6.5 89.9 %copy-start = (bf16[512,64]{0,1:T(8,128)(2,1)S(1)}, bf16[512,64]{0,1:T(8,128)(2,1)}, u32[]{:S(2)}) copy-start(bf16[512,64]{0,1:T(8,128)(2,1)} %param.12) | copy-start | bytes 196612
  6.5 26.4 %copy-start.4 = (bf16[2,64,128]{2,1,0:T(8,128)(2,1)S(1)}, bf16[2,64,128]{2,1,0:T(8,128)(2,1)}, u32[]{:S(2)}) copy-start(bf16[2,64,128]{2,1,0:T(8,128)(2,1)} %param.9) | copy-start | bytes 98308
  6.5 26.4 %copy-start.2 = (bf16[2,64,1024]{2,1,0:T(8,128)(2,1)S(1)}, bf16[2,64,1024]{2,1,0:T(8,128)(2,1)}, u32[]{:S(2)}) copy-start(bf16[2,64,1024]{2,1,0:T(8,128)(2,1)} %param.11) | copy-start | bytes 786436
  6.5 215.9 %all-reduce.10.cloned.1.call-start = ((), (), s32[]{:S(2)}) async-start(), calls=%async_computation | async-start | bytes 1048576 | tf_op jit(solution)/shard_map/psum | solution.py:82
  51.8 5.4 %collective-permute-start.1 = (bf16[2,64,128]{2,1,0:T(8,128)(2,1)S(1)}, bf16[2,64,128]{2,1,0:T(8,128)(2,1)S(1)}, u32[]{:S(2)}, u32[]{:S(2)}) collective-permute-start(bf16[2,64,128]{2,1,0:T(8,128)(2,1)S(1)} %fusion.54), channel_id=1, source_target_pairs={{0,128},{1,129},{2,130},{3,131},{4,132},{5,133},{6,134},{7,135},{8... | collective-permute-start | bytes 98312 | tf_op jit(solution)/shard_map/ppermute | solution.py:13
  77.8 20.1 %copy-start.7 = (s32[1,16]{1,0:T(1,128)S(1)}, s32[1,16]{1,0:T(1,128)}, u32[]{:S(2)}) copy-start(s32[1,16]{1,0:T(1,128)} %param.15) | copy-start | bytes 196
  96.3 129.2 %copy-start.3 = (f32[7]{0:T(128)S(1)}, f32[7]{0:T(128)}, u32[]{:S(2)}) copy-start(f32[7]{0:T(128)} %param.13) | copy-start | bytes 88
  96.3 166.5 %copy-start.1 = (bf16[2048,512]{1,0:T(8,128)(2,1)S(1)}, bf16[2048,512]{1,0:T(8,128)(2,1)}, u32[]{:S(2)}) copy-start(bf16[2048,512]{1,0:T(8,128)(2,1)} %param.14) | copy-start | bytes 6291460
  97.8 164.9 %all-reduce.12.cloned.1.call-start = ((), (), s32[]{:S(2)}) async-start(), calls=%async_computation.1 | async-start | bytes 524288 | tf_op jit(solution)/shard_map/psum | solution.py:18
  264.4 8.3 %copy-start.5 = (bf16[2,512,128]{1,2,0:T(8,128)(2,1)S(1)}, bf16[2,512,128]{1,2,0:T(8,128)(2,1)}, u32[]{:S(2)}) copy-start(bf16[2,512,128]{1,2,0:T(8,128)(2,1)} %all-reduce.12.cloned.1.call-done) | copy-start | bytes 786436
  272.8 8.6 %collective-permute-start = (bf16[2,512,128]{1,2,0:T(8,128)(2,1)S(1)}, bf16[2,512,128]{1,2,0:T(8,128)(2,1)S(1)}, u32[]{:S(2)}, u32[]{:S(2)}) collective-permute-start(bf16[2,512,128]{1,2,0:T(8,128)(2,1)S(1)} %get-tuple-element.536), channel_id=1, source_target_pairs={{7,0},{0,1},{1,2},{2,3},{3,4},{4,5},{5,6},{6,7},{15,8},{8,9},{9,10... | collective-permute-start | bytes 786440 | tf_op jit(solution)/shard_map/while/body/eval_jaxpr/ppermute | solution.py:24
  290.5 7.3 %collective-permute-start = (bf16[2,512,128]{1,2,0:T(8,128)(2,1)S(1)}, bf16[2,512,128]{1,2,0:T(8,128)(2,1)S(1)}, u32[]{:S(2)}, u32[]{:S(2)}) collective-permute-start(bf16[2,512,128]{1,2,0:T(8,128)(2,1)S(1)} %get-tuple-element.536), channel_id=1, source_target_pairs={{7,0},{0,1},{1,2},{2,3},{3,4},{4,5},{5,6},{6,7},{15,8},{8,9},{9,10... | collective-permute-start | bytes 786440 | tf_op jit(solution)/shard_map/while/body/eval_jaxpr/ppermute | solution.py:24
  307.0 6.5 %collective-permute-start = (bf16[2,512,128]{1,2,0:T(8,128)(2,1)S(1)}, bf16[2,512,128]{1,2,0:T(8,128)(2,1)S(1)}, u32[]{:S(2)}, u32[]{:S(2)}) collective-permute-start(bf16[2,512,128]{1,2,0:T(8,128)(2,1)S(1)} %get-tuple-element.536), channel_id=1, source_target_pairs={{7,0},{0,1},{1,2},{2,3},{3,4},{4,5},{5,6},{6,7},{15,8},{8,9},{9,10... | collective-permute-start | bytes 786440 | tf_op jit(solution)/shard_map/while/body/eval_jaxpr/ppermute | solution.py:24
  322.6 6.5 %collective-permute-start = (bf16[2,512,128]{1,2,0:T(8,128)(2,1)S(1)}, bf16[2,512,128]{1,2,0:T(8,128)(2,1)S(1)}, u32[]{:S(2)}, u32[]{:S(2)}) collective-permute-start(bf16[2,512,128]{1,2,0:T(8,128)(2,1)S(1)} %get-tuple-element.536), channel_id=1, source_target_pairs={{7,0},{0,1},{1,2},{2,3},{3,4},{4,5},{5,6},{6,7},{15,8},{8,9},{9,10... | collective-permute-start | bytes 786440 | tf_op jit(solution)/shard_map/while/body/eval_jaxpr/ppermute | solution.py:24
  338.2 6.5 %collective-permute-start = (bf16[2,512,128]{1,2,0:T(8,128)(2,1)S(1)}, bf16[2,512,128]{1,2,0:T(8,128)(2,1)S(1)}, u32[]{:S(2)}, u32[]{:S(2)}) collective-permute-start(bf16[2,512,128]{1,2,0:T(8,128)(2,1)S(1)} %get-tuple-element.536), channel_id=1, source_target_pairs={{7,0},{0,1},{1,2},{2,3},{3,4},{4,5},{5,6},{6,7},{15,8},{8,9},{9,10... | collective-permute-start | bytes 786440 | tf_op jit(solution)/shard_map/while/body/eval_jaxpr/ppermute | solution.py:24
  353.9 6.5 %collective-permute-start = (bf16[2,512,128]{1,2,0:T(8,128)(2,1)S(1)}, bf16[2,512,128]{1,2,0:T(8,128)(2,1)S(1)}, u32[]{:S(2)}, u32[]{:S(2)}) collective-permute-start(bf16[2,512,128]{1,2,0:T(8,128)(2,1)S(1)} %get-tuple-element.536), channel_id=1, source_target_pairs={{7,0},{0,1},{1,2},{2,3},{3,4},{4,5},{5,6},{6,7},{15,8},{8,9},{9,10... | collective-permute-start | bytes 786440 | tf_op jit(solution)/shard_map/while/body/eval_jaxpr/ppermute | solution.py:24
  369.5 6.5 %collective-permute-start = (bf16[2,512,128]{1,2,0:T(8,128)(2,1)S(1)}, bf16[2,512,128]{1,2,0:T(8,128)(2,1)S(1)}, u32[]{:S(2)}, u32[]{:S(2)}) collective-permute-start(bf16[2,512,128]{1,2,0:T(8,128)(2,1)S(1)} %get-tuple-element.536), channel_id=1, source_target_pairs={{7,0},{0,1},{1,2},{2,3},{3,4},{4,5},{5,6},{6,7},{15,8},{8,9},{9,10... | collective-permute-start | bytes 786440 | tf_op jit(solution)/shard_map/while/body/eval_jaxpr/ppermute | solution.py:24
  385.1 0.6 copy-start.6
Sparse Core Ops, SparseCore 0:
  98.0 124.4 all-reduce.9
  225.6 37.1 all-reduce.11
where the time goes:
time: 400 us; the launch traced here: 393 us
  waiting for transfers between devices  203 us (51%)
  blocking collectives  77.9 us (19%)
  other arithmetic  70.2 us (18%)
  between operations  14.4 us (4%)
  matrix products  11.6 us (3%)
  local copies, waits for them, and re-layouts  8.88 us (2%)
  starting transfers between devices  6.25 us (2%)
    psum x1, waiting for transfers between devices, per_device(): summed_all = lax.psum(projected, 'bank')  124 us
    all_gather x4, blocking collectives, encode_layer(): piece_rows = lax.all_gather(activated, 'bank', axis=1, tiled=True)  77.9 us
    reduce_max x16, other arithmetic, score(): jnp.max(filtered.reshape(rows, frames_per_clip, tile_count, TILE), axis=(...  66.2 us
    ppermute x7, waiting for transfers between devices, shifted(): return lax.ppermute(block, axis, route)  41.9 us
    psum x1, waiting for transfers between devices, broadcast(): return lax.psum(block, axis)  35.9 us
  transfers between devices with their start and end apart: 10, of which 10 were waited for; matrix products, arithmetic and copies ran while one was open for 1% of the time, Pallas kernels for 0%

commit v1 on v0

v1 whole, which is shorter than its diff:
```python
import functools

import jax
import jax.numpy as jnp
from jax import lax
from jax.experimental import pallas as pl
from jax.experimental.pallas import tpu as pltpu
from jax.sharding import PartitionSpec as P

BF = jnp.bfloat16
F32 = jnp.float32
TAPS = 7
SUB = 8
PAD = 4
STEPS = 4
GROUP = 8


def kernel(
    G, Z, q_ref, cw_ref, mw_ref, pw_ref, taps_ref, rf_ref, sl_ref, out_ref,
    wmix, wconv, wown, wsib, wproj, hin, hout, U, D, rbuf, r32, rperm, wtab, s0, s1, acc,
    loc, sib_s, sib_r, gat_s, gat_r, ph_s, ph_r, ring_s, ring_r,
):
    half_ch = q_ref.shape[1]
    ch = 2 * half_ch
    T = q_ref.shape[2]
    C = mw_ref.shape[2]
    E = pw_ref.shape[0]
    F = rf_ref.shape[0]
    slices = sl_ref.shape[1]
    gw = cw_ref.shape[3]
    LO = F // SUB
    rows_all = (LO + 2 * PAD) * SUB
    per_step = (LO + 2 * PAD) // STEPS
    out_step = LO // STEPS

    phase = lax.axis_index("phase")
    bank = lax.axis_index("bank")
    blk = lax.axis_index("blk")
    core = lax.rem(bank, 2)
    chip = bank // 2
    me_sib = (phase, chip * 2 + 1 - core, blk)
    me_next = (1 - phase, bank, blk)
    me_cross = (1 - phase, lax.rem(chip + G // 2, G) * 2 + core, blk)
    up = (phase, bank, lax.rem(blk + 1, Z))
    down = (phase, bank, lax.rem(blk + Z - 1, Z))

    def peer(o):
        return lax.rem(chip + o, G)

    def chip_dev(c):
        return (phase, c * 2 + core, blk)

    barrier = pltpu.get_barrier_semaphore()
    greet = [me_sib, me_next, me_cross, up, down] + [chip_dev(peer(o)) for o in range(1, G)]
    for dev in greet:
        pl.semaphore_signal(
            barrier, inc=1, device_id=dev, device_id_type=pl.DeviceIdType.MESH
        )

    def rc(src, dst, ssem, rsem, dev):
        return pltpu.make_async_remote_copy(
            src_ref=src, dst_ref=dst, send_sem=ssem, recv_sem=rsem,
            device_id=dev, device_id_type=pl.DeviceIdType.MESH,
        )

    mine = pl.ds(pl.multiple_of(core * half_ch, half_ch), half_ch)

    def chip_rows(c):
        return pl.ds(pl.multiple_of(c * ch, ch), ch)

    load_r = pltpu.make_async_copy(rf_ref, rbuf, loc.at[0])
    load_r.start()
    load_m = pltpu.make_async_copy(mw_ref, wmix.at[:, mine], loc.at[1])
    load_m.start()

    lane = lax.broadcasted_iota(jnp.int32, (half_ch, ch), 1)
    row = lax.broadcasted_iota(jnp.int32, (half_ch, ch), 0)
    block = (lane // gw) == (row // gw + core * (half_ch // gw))
    spread = (
        lax.broadcasted_iota(jnp.int32, (gw, ch), 1) % gw
        == lax.broadcasted_iota(jnp.int32, (gw, ch), 0)
    ).astype(F32).astype(BF)
    for l in range(2):
        for k in range(3):
            wide = jnp.dot(cw_ref[l, k], spread, preferred_element_type=F32)
            wconv[l, mine, k * ch : (k + 1) * ch] = jnp.where(block, wide, 0.0).astype(BF)
    move = (
        lax.broadcasted_iota(jnp.int32, (half_ch, ch), 1)
        == lax.broadcasted_iota(jnp.int32, (half_ch, ch), 0) + core * half_ch
    ).astype(F32).astype(BF)
    wown[...] = jnp.dot(pw_ref[...], move, preferred_element_type=F32).astype(BF)

    pl.semaphore_wait(barrier, len(greet))

    first = phase == 0
    second = phase == 1

    c_conv = rc(wconv.at[:, mine], wconv.at[:, mine], sib_s.at[0], sib_r.at[0], me_sib)
    c_mix = rc(mw_ref, wmix.at[:, mine], sib_s.at[1], sib_r.at[1], me_sib)
    c_q = rc(q_ref.at[1 - core], hin.at[mine], sib_s.at[2], sib_r.at[2], me_sib)
    c_h = rc(hout, hin, ph_s.at[0], ph_r.at[0], me_next)
    c_d = rc(D.at[blk, core], D.at[blk, core], ph_s.at[1], ph_r.at[1], me_cross)
    eh = E // 2
    my_e = pl.ds(pl.multiple_of(core * eh, eh), eh)
    its_e = pl.ds(pl.multiple_of((1 - core) * eh, eh), eh)
    c_own = rc(wown.at[its_e], wsib.at[its_e], sib_s.at[3], sib_r.at[3], me_sib)
    c_wp = rc(wproj.at[my_e], wproj.at[my_e], sib_s.at[4], sib_r.at[4], me_sib)

    def chip_cols(c):
        return pl.ds(pl.multiple_of(c * ch, ch), ch)

    def push_proj(o):
        part = wproj.at[my_e, chip_cols(chip)]
        return rc(part, part, gat_s.at[3, o], gat_r.at[3, chip], chip_dev(peer(o)))

    @pl.when(first)
    def _():
        c_q.start()
        hin[mine] = q_ref[core]

    c_conv.start()
    c_mix.start()

    @pl.when(second)
    def _():
        c_own.start()
        c_own.wait_recv()
        wproj[my_e, chip_cols(chip)] = wown[my_e] + wsib[my_e]
        for o in range(1, G):
            push_proj(o).start()

    def gather(l, value):
        U[l, chip_rows(chip)] = value
        for o in range(1, G):
            part = U.at[l, chip_rows(chip)]
            rc(part, part, gat_s.at[l, o], gat_r.at[l, chip], chip_dev(peer(o))).start()
        for o in range(1, G):
            c = peer(o)
            part = U.at[l, chip_rows(c)]
            rc(part, part, gat_s.at[l, o], gat_r.at[l, c], chip_dev(c)).wait_recv()

    def encode():
        @pl.when(first)
        def _():
            c_q.wait_recv()

        @pl.when(second)
        def _():
            c_h.wait_recv()

        c_conv.wait_recv()
        frame = lax.broadcasted_iota(jnp.int32, (ch, T), 1)
        h = hin[...].astype(F32)
        for l in range(2):
            d = jnp.left_shift(jnp.int32(1), phase * 2 + l)
            before = jnp.where(frame >= d, pltpu.roll(h, d, 1), 0.0)
            after = jnp.where(frame < T - d, pltpu.roll(h, T - d, 1), 0.0)
            x = jnp.concatenate([before, h, after], axis=0).astype(BF)
            a = jnp.dot(wconv[l], x, preferred_element_type=F32)
            gather(l, jax.nn.gelu(a, approximate=True).astype(BF))
            if l == 0:
                load_m.wait()
                c_mix.wait_recv()
            u = U[l]
            m = jnp.dot(wmix[l], u, preferred_element_type=F32)
            uf = u.astype(F32)
            sq = jnp.sum(uf * uf, axis=0, keepdims=True)
            h = (h + m * lax.rsqrt(sq / C + 1e-6)).astype(BF).astype(F32)

        @pl.when(first)
        def _():
            hout[...] = h.astype(BF)
            c_h.start()

        @pl.when(second)
        def _():
            gather(2, h.astype(BF))
            c_wp.wait_recv()
            p = jnp.dot(wproj[...], U[2], preferred_element_type=F32)
            norm = lax.rsqrt(jnp.sum(p * p, axis=0, keepdims=True) / E + 1e-6)
            D[blk, core] = (p * norm).astype(BF)
            c_d.start()

    def prepare():
        @pl.when(second)
        def _():
            for o in range(1, G):
                c = peer(o)
                part = wproj.at[my_e, chip_cols(c)]
                rc(part, part, gat_s.at[3, o], gat_r.at[3, c], chip_dev(c)).wait_recv()
            c_wp.start()

        load_r.wait()
        lanes = E // T
        r32[:, 0:8] = jnp.zeros((lanes, 8, T), F32)
        r32[:, F + 8 : F + 16] = jnp.zeros((lanes, 8, T), F32)

        @pl.loop(0, F // 64)
        def _(i):
            at = pl.multiple_of(i * 64, 64)
            for b in range(lanes):
                piece = rbuf[pl.ds(at, 64), b * T : (b + 1) * T]
                r32[b, pl.ds(at + 8, 64)] = piece.astype(F32)

        @pl.loop(0, (LO + 2 * PAD) // 4)
        def _(i):
            for k in range(2):
                at = i * 4 + k * 2 + 8 - PAD
                to = pl.multiple_of(i * 32 + k * 16, 16)
                for b in range(lanes):
                    two = jnp.concatenate(
                        [r32[b, pl.ds(at + v, SUB, stride=LO), :] for v in range(2)], axis=0
                    )
                    rperm[pl.ds(to, 16), b * T : (b + 1) * T] = two.astype(BF)

        ends = []
        total = jnp.int32(0)
        for k in range(slices):
            total = total + sl_ref[0, k]
            ends.append(total)
        scale = E ** (-0.5)

        @pl.loop(0, LO // 8)
        def _(i):
            shape = (8, SUB, T)
            lo = lax.broadcasted_iota(jnp.int32, shape, 0) + i * 8
            r = lax.broadcasted_iota(jnp.int32, shape, 1) * LO + lo
            begin = jnp.zeros(shape, jnp.int32)
            end = jnp.full(shape, F, jnp.int32)
            for e in ends:
                begin = jnp.maximum(begin, jnp.where(r >= e, e, 0))
                end = jnp.minimum(end, jnp.where(r < e, e, F))
            t = (lax.broadcasted_iota(jnp.int32, shape, 2) + lo) & (T - 1)
            at = pl.ds(i * 8, 8)
            for k in range(TAPS):
                j = k - TAPS // 2
                inside = jnp.where((r + j >= begin) & (r + j < end), taps_ref[k] * scale, 0.0)
                wtab[k, at] = jnp.where((t + j >= 0) & (t + j < T), inside, 0.0)

        acc[...] = jnp.full(acc.shape, -jnp.inf, F32)

    @pl.loop(0, 2)
    def _(turn):
        pl.when(turn == phase)(encode)
        pl.when(turn == 0)(prepare)

    @pl.when(first)
    def _():
        c_d.wait_recv()

    def multiply(z, c, into):
        both = jnp.concatenate([D[z, 0], D[z, 1]], axis=1)
        rows = pl.ds(pl.multiple_of(c * (per_step * SUB), 16), per_step * SUB)
        s = jnp.dot(rperm[rows], both, preferred_element_type=F32)
        for i in range(per_step):
            turn = lax.rem(2 * LO + PAD - c * per_step - i, T)
            for n in range(2):
                piece = s[i * SUB : (i + 1) * SUB, n * T : (n + 1) * T]
                into[n, c * per_step + i] = pltpu.roll(piece, turn, 1)

    def select(z, c, s):
        best = [None, None]
        for g in range(out_step // GROUP):
            lo = c * out_step + g * GROUP
            w = [wtab[k, pl.ds(lo, GROUP)] for k in range(TAPS)]
            for n in range(2):
                win = s[n, pl.ds(lo + PAD - 3, GROUP + 6)]
                f = w[0] * win[0:GROUP]
                for k in range(1, TAPS):
                    f = f + w[k] * win[k : k + GROUP]
                f = jnp.max(f, axis=0)
                best[n] = f if best[n] is None else jnp.maximum(best[n], f)
        for n in range(2):
            at = (z * 2 + n) * 2 + c // (STEPS // 2)
            acc[at] = jnp.maximum(acc[at], best[n])

    def run(new, into, old, held):
        @pl.loop(0, STEPS)
        def _(c):
            if old is not None:
                select(old, c, held)
            if new is not None:
                multiply(new, c, into)

    def slot(shift):
        return lax.rem(blk + Z + shift, Z)

    H = Z // 2

    def ring(way, step):
        z = slot((1 - way * 2) * (1 - step))
        ref = D.at[z, core]
        return rc(ref, ref, ring_s.at[way, step], ring_r.at[way, step], (up, down)[way])

    def ring_last(way):
        z = slot((1 - way * 2) * (1 - H))
        ref = D.at[z, core, way * eh : (way + 1) * eh]
        return rc(ref, ref, ring_s.at[way, H], ring_r.at[way, H], (up, down)[way])

    def arrival(way, step):
        ref = D.at[slot((way * 2 - 1) * step), core]
        return rc(ref, ref, ring_s.at[way, step], ring_r.at[way, step], (up, down)[way])

    def arrival_last(way):
        ref = D.at[slot(H), core, way * eh : (way + 1) * eh]
        return rc(ref, ref, ring_s.at[way, H], ring_r.at[way, H], (up, down)[way])

    def hand(z):
        ref = D.at[z, core]
        return rc(ref, ref, sib_s.at[5 + z], sib_r.at[5 + z], me_sib)

    def handed(z):
        ref = D.at[z, 1 - core]
        return rc(ref, ref, sib_s.at[5 + z], sib_r.at[5 + z], me_sib)

    hand(blk).start()
    for way in range(2):
        if H > 1:
            ring(way, 1).start()
        else:
            ring_last(way).start()
    handed(blk).wait_recv()
    run(blk, s1, None, None)

    if H > 1:
        @pl.loop(1, H)
        def _(step):
            for way in range(2):
                arrival(way, step).wait_recv()

                @pl.when(step < H - 1)
                def _():
                    ring(way, step + 1).start()

                @pl.when(step == H - 1)
                def _():
                    ring_last(way).start()

                hand(slot((way * 2 - 1) * step)).start()
            for way in range(2):
                z = slot((way * 2 - 1) * step)
                handed(z).wait_recv()
                prev = slot(-step) if way else slot(step - 1)
                run(z, (s0, s1)[way], prev, (s1, s0)[way])

    for way in range(2):
        arrival_last(way).wait_recv()
    hand(slot(H)).start()
    handed(slot(H)).wait_recv()
    run(slot(H), s0, slot(H - 1), s1)
    run(None, None, slot(H), s0)

    out_ref[...] = jnp.max(
        acc[...].reshape(Z * 4 * SUB, T).T, axis=0, keepdims=True
    )

    c_conv.wait_send()
    c_mix.wait_send()

    @pl.when(first)
    def _():
        c_q.wait_send()
        c_h.wait_send()

    @pl.when(second)
    def _():
        c_own.wait_send()
        c_wp.wait_send()
        c_d.wait_send()
        for o in range(1, G):
            push_proj(o).wait_send()
            part = U.at[2, chip_rows(chip)]
            rc(part, part, gat_s.at[2, o], gat_r.at[2, chip], chip_dev(peer(o))).wait_send()

    for l in range(2):
        for o in range(1, G):
            part = U.at[l, chip_rows(chip)]
            rc(part, part, gat_s.at[l, o], gat_r.at[l, chip], chip_dev(peer(o))).wait_send()
    for way in range(2):
        for step in range(1, H):
            ring(way, step).wait_send()
        ring_last(way).wait_send()
    for z in range(Z):
        hand(z).wait_send()


def solution(mesh):
    G = mesh.shape["bank"] // 2
    Z = mesh.shape["blk"]

    def per_device(q, cw, mw, pw, taps, rf, sl):
        half_ch, T = q.shape[1:]
        ch = 2 * half_ch
        C = mw.shape[2]
        E = pw.shape[0]
        F = rf.shape[0]
        LO = F // SUB
        dma = pltpu.SemaphoreType.DMA
        vmem = pl.BlockSpec(memory_space=pltpu.VMEM)
        smem = pl.BlockSpec(memory_space=pltpu.SMEM)
        anyw = pl.BlockSpec(memory_space=pl.ANY)
        maxima = pl.pallas_call(
            functools.partial(kernel, G, Z),
            out_shape=jax.ShapeDtypeStruct((1, Z * 4 * SUB), F32),
            in_specs=[vmem, vmem, anyw, vmem, smem, anyw, smem],
            out_specs=vmem,
            scratch_shapes=[
                pltpu.VMEM((2, ch, C), BF),
                pltpu.VMEM((2, ch, 3 * ch), BF),
                pltpu.VMEM((E, ch), BF),
                pltpu.VMEM((E, ch), BF),
                pltpu.VMEM((E, C), BF),
                pltpu.VMEM((ch, T), BF),
                pltpu.VMEM((ch, T), BF),
                pltpu.VMEM((3, C, T), BF),
                pltpu.VMEM((Z, 2, E, T), BF),
                pltpu.VMEM((F, E), BF),
                pltpu.VMEM((E // T, F + 16, T), F32),
                pltpu.VMEM(((LO + 2 * PAD) * SUB, E), BF),
                pltpu.VMEM((TAPS, LO, SUB, T), F32),
                pltpu.VMEM((2, LO + 2 * PAD, SUB, T), F32),
                pltpu.VMEM((2, LO + 2 * PAD, SUB, T), F32),
                pltpu.VMEM((Z * 4, SUB, T), F32),
                dma((2,)),
                dma((5 + Z,)),
                dma((5 + Z,)),
                dma((4, G)),
                dma((4, G)),
                dma((2,)),
                dma((2,)),
                dma((2, Z // 2 + 1)),
                dma((2, Z // 2 + 1)),
            ],
            compiler_params=pltpu.CompilerParams(
                collective_id=0,
                has_side_effects=True,
                vmem_limit_bytes=48 * 1024 * 1024,
            ),
        )(q, cw, mw, pw, taps, rf, sl)
        maxima = maxima.reshape(2 * Z, 2, SUB)
        return jnp.transpose(maxima, (0, 2, 1)).reshape(2 * Z, 2 * SUB)

    return jax.shard_map(
        per_device,
        mesh=mesh,
        in_specs=(
            P("blk", "bank", None),
            P("phase", None, "bank", None),
            P("phase", "bank", None),
            P(None, "bank"),
            P(),
            P(("phase", "bank", "blk"), None),
            P(("phase", "bank", "blk"), None),
        ),
        out_specs=P(None, ("phase", "bank", "blk")),
        check_vma=False,
    )
```

time: 400 us -> 86.8 us (0.22); the launches traced: 393 us -> 86.5 us
  waiting for transfers between devices: 203 us -> 0 us
  Pallas kernels: 0 us -> 78 us
  blocking collectives: 77.9 us -> 0 us
  other arithmetic: 70.2 us -> 0.66 us
  between operations: 14.4 us -> 0.04 us
  matrix products: 11.6 us -> 0 us
  starting transfers between devices: 6.25 us -> 0 us
    psum x2 -> x0, waiting for transfers between devices: 160 us -> none  [the longest x1 124 us: per_device(): summed_all = lax.psum(projected, 'bank')]
    pallas_call x0 -> x1, Pallas kernels: none -> 78 us  [per_device(): pl.pallas_call(functools.partial(kernel, G, Z), out_shape=jax.ShapeDtypeS...]
    all_gather x4 -> x0, blocking collectives: 77.9 us -> none  [encode_layer(): piece_rows = lax.all_gather(activated, 'bank', axis=1, tiled=True)]
    reduce_max x16 -> x0, other arithmetic: 66.2 us -> none  [score(): jnp.max(filtered.reshape(rows, frames_per_clip, tile_count, TILE), axis=(...]
    ppermute x8 -> x0, waiting for transfers between devices: 42.9 us -> none  [the longest x7 41.9 us: shifted(): return lax.ppermute(block, axis, route)]
    dot_general x24 -> x0, matrix products: 11.6 us -> none  [the longest x8 7.23 us: score(): jnp.einsum('bet,re->btr', panel_now, reference_frames, preferred_element_...]
    slice x15 -> x0, local copies, waits for them, and re-layouts: 6.68 us -> none  [the longest x8 5.28 us: score(): taps[shift_index]]
    ppermute x8 -> x0, starting transfers between devices: 6.21 us -> none  [the longest x1 4.36 us: from_behind(): return lax.ppermute(value, axis, pairs)]
  transfers between devices with their start and end apart: 10 -> 0, of which waited for: 10 -> 0; matrix products, arithmetic and copies ran while one was open for 1% -> 0% of each run, Pallas kernels for 0% -> 0%
where the time goes in v1:
time: 86.8 us; the launch traced here: 86.5 us
  Pallas kernels  78 us (90%)
  local copies, waits for them, and re-layouts  7.84 us (9%)
    pallas_call x1, Pallas kernels, per_device(): pl.pallas_call(functools.partial(kernel, G, Z), out_shape=jax.ShapeDtypeS...  78 us
    unnamed x12, local copies, waits for them, and re-layouts  6.48 us

profile of v1, /device:TPU:1, one launch (start us, length us, event | category | flops | bytes accessed | tf_op | source)
XLA Modules:
  0.0 86.5 jit_solution(4977038867600103627)
XLA Ops:
  0.0 1.0 %copy.12.pw_ref = bf16[512,64]{1,0:T(8,128)(2,1)S(1)} copy(bf16[512,64]{0,1:T(8,128)(2,1)} %param.10) | data formatting | bytes 131072 | tf_op args[3]
  1.0 0.9 %copy.11.cw_ref = bf16[2,3,64,32]{3,2,1,0:T(8,128)(2,1)S(1)} copy(bf16[2,3,64,32]{2,3,1,0:T(8,128)(2,1)} %param.8) | data formatting | bytes 49152 | tf_op args[1]
  1.9 0.0 copy-start
  1.9 1.6 %copy-done = bf16[2048,512]{1,0:T(8,128)(2,1)S(1)} copy-done((bf16[2048,512]{1,0:T(8,128)(2,1)S(1)}, bf16[2048,512]{1,0:T(8,128)(2,1)}, u32[]{:S(2)}) %copy-start) | copy-done | bytes 2097176
  3.5 0.0 copy-start.1
  3.5 0.9 %copy-done.1 = bf16[2,64,1024]{2,1,0:T(8,128)(2,1)S(1)} copy-done((bf16[2,64,1024]{2,1,0:T(8,128)(2,1)S(1)}, bf16[2,64,1024]{2,1,0:T(8,128)(2,1)}, u32[]{:S(2)}) %copy-start.1) | copy-done | bytes 262168
  4.4 0.0 copy-start.2
  4.4 0.8 copy-done.2
  5.2 0.0 copy-start.3
  5.2 0.7 copy-done.3
  5.8 0.0 copy-start.4
  5.8 0.7 copy-done.4
  6.5 78.0 %shard_map.73 = f32[1,256]{1,0:T(1,128)S(1)} custom-call(bf16[2,64,128]{2,1,0:T(8,128)(2,1)S(1)} %copy-done.2, bf16[2,3,64,32]{3,2,1,0:T(8,128)(2,1)S(1)} %copy.11.cw_ref, bf16[2,64,1024]{2,1,0:T(8,128)(2,1)S(1)} %copy-done.1, bf16[512,64]{1,0:T(8,128)(2,1)S(1)} %copy.12.pw_ref, f32[7]{0:T(128)S(1)} %copy-done.3, bf16[2048,512]{1,0:T(8,128)(2,1)S(1)} %copy-done, ...), custom_call_target="tpu_custom_call" | custom-call | tf_op jit(solution)/shard_map/pallas_call | solution.py:403
  84.5 0.5 broadcast.3
  85.0 0.7 reduce.3
  85.6 0.1 reshape.6
  85.7 0.1 copy.13
  85.8 0.7 copy.14
Async XLA Ops:
  1.9 1.6 %copy-start = (bf16[2048,512]{1,0:T(8,128)(2,1)S(1)}, bf16[2048,512]{1,0:T(8,128)(2,1)}, u32[]{:S(2)}) copy-start(bf16[2048,512]{1,0:T(8,128)(2,1)} %rf_ref.1) | copy-start | bytes 6291460
  3.5 0.9 %copy-start.1 = (bf16[2,64,1024]{2,1,0:T(8,128)(2,1)S(1)}, bf16[2,64,1024]{2,1,0:T(8,128)(2,1)}, u32[]{:S(2)}) copy-start(bf16[2,64,1024]{2,1,0:T(8,128)(2,1)} %mw_ref.1) | copy-start | bytes 786436
  4.4 0.8 copy-start.2
  5.2 0.7 copy-start.3
  5.8 0.7 copy-start.4

commit v2 on v1

v2 whole, which is shorter than its diff:
```python
import functools

import jax
import jax.numpy as jnp
from jax import lax
from jax.experimental import pallas as pl
from jax.experimental.pallas import tpu as pltpu
from jax.sharding import PartitionSpec as P

BF = jnp.bfloat16
F32 = jnp.float32
TAPS = 7
SUB = 8
PAD = 4
STEPS = 4
GROUP = 8


def kernel(
    G, Z, q_hbm, cw_hbm, mw_ref, pw_hbm, taps_ref, rf_ref, sl_ref, out_ref,
    q_ref, cw_ref, pw_ref, wraw, wconv, wfull, wown, wsib, wproj, hin, hout, hall, U, D,
    rbuf, r32, rperm, wtab, s0, s1, acc,
    loc, sib_s, sib_r, gat_s, gat_r, hop_s, hop_r, par_s, par_r, far_s, far_r, row_s, row_r,
):
    half_ch = q_ref.shape[1]
    ch = 2 * half_ch
    T = q_ref.shape[2]
    C = mw_ref.shape[2]
    E = pw_ref.shape[1]
    F = rf_ref.shape[0]
    slices = sl_ref.shape[1]
    gw = cw_ref.shape[2]
    LO = F // SUB
    per_step = (LO + 2 * PAD) // STEPS
    out_step = LO // STEPS
    Y = G // 2
    H = Z // 2

    phase = lax.axis_index("phase")
    bank = lax.axis_index("bank")
    blk = lax.axis_index("blk")
    core = lax.rem(bank, 2)
    chip = bank // 2
    col = chip // Y
    row = lax.rem(chip, Y)
    me_sib = (phase, chip * 2 + 1 - core, blk)
    across = lax.rem(chip + Y, G) * 2 + core
    first = phase == 0
    second = phase == 1

    def peer(o):
        return lax.rem(chip + o, G)

    def chip_dev(c):
        return (phase, c * 2 + core, blk)

    def row_dev(v):
        return (phase, (col * Y + lax.rem(row + v, Y)) * 2 + core, blk)

    def slot(shift):
        return lax.rem(blk + Z + shift, Z)

    load_q = pltpu.make_async_copy(q_hbm, q_ref, loc.at[2])
    load_c = pltpu.make_async_copy(cw_hbm, cw_ref, loc.at[3])
    load_p = pltpu.make_async_copy(pw_hbm, pw_ref, loc.at[4])
    load_c.start()
    load_q.start()
    load_p.start()

    barrier = pltpu.get_barrier_semaphore()
    greet = [me_sib] + [chip_dev(peer(o)) for o in range(1, G)]
    greet += [(phase, bank, slot(o)) for o in range(1, Z)]
    greet += [(1 - phase, across, slot(o)) for o in range(1, Z)]
    greet += [(1 - phase, c * 2 + core, blk) for c in range(G)]
    for dev in greet:
        pl.semaphore_signal(
            barrier, inc=1, device_id=dev, device_id_type=pl.DeviceIdType.MESH
        )

    load_m = pltpu.make_async_copy(mw_ref, wfull.at[:, chip, core], loc.at[1])
    load_m.start()
    load_r = pltpu.make_async_copy(rf_ref, rbuf, loc.at[0])
    load_r.start()

    def rc(src, dst, ssem, rsem, dev):
        return pltpu.make_async_remote_copy(
            src_ref=src, dst_ref=dst, send_sem=ssem, recv_sem=rsem,
            device_id=dev, device_id_type=pl.DeviceIdType.MESH,
        )

    def iota(shape, axis):
        return lax.broadcasted_iota(jnp.int32, shape, axis)

    def ones(mask):
        return mask.astype(F32).astype(BF)

    def turned(a, b):
        return lax.dot_general(a, b, (((0,), (0,)), ((), ())), preferred_element_type=F32)

    def chip_rows(c):
        return pl.ds(pl.multiple_of(c * ch, ch), ch)

    mine = pl.ds(pl.multiple_of(core * half_ch, half_ch), half_ch)
    eh = E // 2
    my_e = pl.ds(pl.multiple_of(core * eh, eh), eh)
    its_e = pl.ds(pl.multiple_of((1 - core) * eh, eh), eh)
    eq = E // Y

    def part_e(r):
        return pl.ds(pl.multiple_of(r * eq, eq), eq)

    load_c.wait()
    for l in range(2):
        flat = None
        for k in range(3):
            put = ones(iota((gw, T), 1) == iota((gw, T), 0) + k * gw)
            wide = turned(cw_ref[l, k], put)
            flat = wide if flat is None else flat + wide
        wraw[l, chip, core] = flat.astype(BF)
    load_q.wait()

    pl.semaphore_wait(barrier, len(greet))

    c_conv = rc(
        wraw.at[:, chip, core], wraw.at[:, chip, core], sib_s.at[0], sib_r.at[0], me_sib
    )
    c_mix = rc(mw_ref, wfull.at[:, chip, core], sib_s.at[1], sib_r.at[1], me_sib)
    c_q = rc(q_ref.at[1 - core], hin.at[mine], sib_s.at[2], sib_r.at[2], me_sib)
    c_own = rc(wown.at[its_e], wsib.at[its_e], sib_s.at[3], sib_r.at[3], me_sib)
    c_wp = rc(wproj.at[my_e], wproj.at[my_e], sib_s.at[4], sib_r.at[4], me_sib)
    c_conv_all = rc(wraw.at[:, :, core], wraw.at[:, :, core], sib_s.at[5], sib_r.at[5], me_sib)

    def c_mix_all(l):
        return rc(
            wfull.at[l, :, core], wfull.at[l, :, core], sib_s.at[6 + l], sib_r.at[6 + l], me_sib
        )

    def push(kind, o, c):
        if kind == 0:
            src = dst = wraw.at[:, c, core]
        elif kind == 3:
            src = dst = wproj.at[my_e, chip_rows(c)]
        else:
            src, dst = mw_ref.at[kind - 1], wfull.at[kind - 1, c, core]
        return rc(src, dst, par_s.at[kind, o], par_r.at[kind, c], chip_dev(peer(o)))

    spread = ones(
        (iota((T, 3 * ch), 0) // gw == iota((T, 3 * ch), 1) // ch)
        & (iota((T, 3 * ch), 0) % gw == iota((T, 3 * ch), 1) % gw)
    )
    block = iota((ch, 3 * ch), 1) % ch // gw == iota((ch, 3 * ch), 0) // gw

    def expand(raw):
        wide = jnp.dot(raw.reshape(ch, T), spread, preferred_element_type=F32)
        return jnp.where(block, wide, 0.0).astype(BF)

    def shifts(h, d):
        frame = iota(h.shape, 1)
        before = jnp.where(frame >= d, pltpu.roll(h, d, 1), 0.0)
        after = jnp.where(frame < T - d, pltpu.roll(h, T - d, 1), 0.0)
        return before.astype(BF), h.astype(BF), after.astype(BF)

    def mixed(h, w, u):
        m = jnp.dot(w, u, preferred_element_type=F32)
        uf = u.astype(F32)
        sq = jnp.sum(uf * uf, axis=0, keepdims=True)
        return (h + m * lax.rsqrt(sq / C + 1e-6)).astype(BF)

    def encode_first():
        c_q.start()
        c_conv.start()
        c_mix.start()
        hin[mine] = q_ref[core]
        c_q.wait_recv()
        c_conv.wait_recv()
        h = hin[...].astype(F32)
        for l in range(2):
            wide = expand(wraw[l, chip])
            x = jnp.concatenate(shifts(h, 1 << l), axis=0)
            a = jnp.dot(wide, x, preferred_element_type=F32)
            part = U.at[l, chip_rows(chip)]
            part[...] = jax.nn.gelu(a, approximate=True).astype(BF)
            for o in range(1, G):
                rc(part, part, gat_s.at[l, o], gat_r.at[l, chip], chip_dev(peer(o))).start()
            if l == 0:
                load_m.wait()
                c_mix.wait_recv()
            for o in range(1, G):
                c = peer(o)
                other = U.at[l, chip_rows(c)]
                rc(other, other, gat_s.at[l, o], gat_r.at[l, c], chip_dev(c)).wait_recv()
            h = mixed(h, wfull[l, chip].reshape(ch, C), U[l]).astype(F32)
        hout[...] = h.astype(BF)
        for c in range(G):
            hop(c).start()
        load_p.wait()

    def hop(c):
        return rc(hout, hall.at[chip], hop_s.at[c], hop_r.at[chip], (1, c * 2 + core, blk))

    def fetch():
        for kind in range(3):
            for o in range(1, G):
                push(kind, o, chip).start()
        load_p.wait()
        move = ones(iota((half_ch, ch), 1) == iota((half_ch, ch), 0) + core * half_ch)
        wown[...] = turned(pw_ref[...], move).astype(BF)
        c_own.start()
        c_own.wait_recv()
        wproj[my_e, chip_rows(chip)] = wown[my_e] + wsib[my_e]
        for o in range(1, G):
            push(3, o, chip).start()

    def encode_second():
        load_m.wait()
        for kind in range(4):
            for o in range(1, G):
                push(kind, o, peer(o)).wait_recv()
            (c_conv_all, c_mix_all(0), c_mix_all(1), c_wp)[kind].start()
        c_conv_all.wait_recv()
        for l in range(2):
            for c in range(G):
                wconv[l, c] = expand(wraw[l, c])
        for c in range(G):
            rc(hout, hall.at[c], hop_s.at[c], hop_r.at[c], me_sib).wait_recv()
        h = hall[...].reshape(C, T).astype(F32)
        for l in range(2):
            sides = shifts(h, 4 << l)
            for c in range(G):
                x = jnp.concatenate([v[c * ch : (c + 1) * ch] for v in sides], axis=0)
                a = jnp.dot(wconv[l, c], x, preferred_element_type=F32)
                U[l, c * ch : (c + 1) * ch] = jax.nn.gelu(a, approximate=True).astype(BF)
            c_mix_all(l).wait_recv()
            h = mixed(h, wfull[l].reshape(C, C), U[l]).astype(F32)
        c_wp.wait_recv()
        p = jnp.dot(wproj[...], h.astype(BF), preferred_element_type=F32)
        norm = lax.rsqrt(jnp.sum(p * p, axis=0, keepdims=True) / E + 1e-6)
        D[blk, core] = (p * norm).astype(BF)

    def prepare():
        load_r.wait()
        lanes = E // T
        r32[:, 0:8] = jnp.zeros((lanes, 8, T), F32)
        r32[:, F + 8 : F + 16] = jnp.zeros((lanes, 8, T), F32)

        @pl.loop(0, F // 64)
        def _(i):
            at = pl.multiple_of(i * 64, 64)
            for b in range(lanes):
                piece = rbuf[pl.ds(at, 64), b * T : (b + 1) * T]
                r32[b, pl.ds(at + 8, 64)] = piece.astype(F32)

        @pl.loop(0, (LO + 2 * PAD) // 4)
        def _(i):
            for k in range(2):
                at = i * 4 + k * 2 + 8 - PAD
                to = pl.multiple_of(i * 32 + k * 16, 16)
                for b in range(lanes):
                    two = jnp.concatenate(
                        [r32[b, pl.ds(at + v, SUB, stride=LO), :] for v in range(2)], axis=0
                    )
                    rperm[pl.ds(to, 16), b * T : (b + 1) * T] = two.astype(BF)

        ends = []
        total = jnp.int32(0)
        for k in range(slices):
            total = total + sl_ref[0, k]
            ends.append(total)
        scale = E ** (-0.5)

        @pl.loop(0, LO // 8)
        def _(i):
            shape = (8, SUB, T)
            lo = lax.broadcasted_iota(jnp.int32, shape, 0) + i * 8
            r = lax.broadcasted_iota(jnp.int32, shape, 1) * LO + lo
            begin = jnp.zeros(shape, jnp.int32)
            end = jnp.full(shape, F, jnp.int32)
            for e in ends:
                begin = jnp.maximum(begin, jnp.where(r >= e, e, 0))
                end = jnp.minimum(end, jnp.where(r < e, e, F))
            t = (lax.broadcasted_iota(jnp.int32, shape, 2) + lo) & (T - 1)
            at = pl.ds(i * 8, 8)
            for k in range(TAPS):
                j = k - TAPS // 2
                inside = jnp.where((r + j >= begin) & (r + j < end), taps_ref[k] * scale, 0.0)
                wtab[k, at] = jnp.where((t + j >= 0) & (t + j < T), inside, 0.0)

        acc[...] = jnp.full(acc.shape, -jnp.inf, F32)

    def multiply(z, c, into):
        both = jnp.concatenate([D[z, 0], D[z, 1]], axis=1)
        rows = pl.ds(pl.multiple_of(c * (per_step * SUB), 16), per_step * SUB)
        s = jnp.dot(rperm[rows], both, preferred_element_type=F32)
        for i in range(per_step):
            turn = lax.rem(2 * LO + PAD - c * per_step - i, T)
            for n in range(2):
                piece = s[i * SUB : (i + 1) * SUB, n * T : (n + 1) * T]
                into[n, c * per_step + i] = pltpu.roll(piece, turn, 1)

    def select(z, c, s):
        best = [None, None]
        for g in range(out_step // GROUP):
            lo = c * out_step + g * GROUP
            w = [wtab[k, pl.ds(lo, GROUP)] for k in range(TAPS)]
            for n in range(2):
                win = s[n, pl.ds(lo + PAD - 3, GROUP + 6)]
                f = w[0] * win[0:GROUP]
                for k in range(1, TAPS):
                    f = f + w[k] * win[k : k + GROUP]
                f = jnp.max(f, axis=0)
                best[n] = f if best[n] is None else jnp.maximum(best[n], f)
        for n in range(2):
            at = (z * 2 + n) * 2 + c // (STEPS // 2)
            acc[at] = jnp.maximum(acc[at], best[n])

    def run(new, into, old, held):
        @pl.loop(0, STEPS)
        def _(c):
            if old is not None:
                select(old, c, held)
            if new is not None:
                multiply(new, c, into)

    def far(o):
        ref = D.at[blk, core, part_e(row)]
        dev = (phase, bank, slot(o)) if o < Z else (1 - phase, across, slot(o - Z))
        return rc(ref, ref, far_s.at[o], far_r.at[blk], dev)

    def far_from(z):
        ref = D.at[z, core, part_e(row)]
        return rc(ref, ref, far_s.at[0], far_r.at[z], me_sib)

    def along(z, v):
        ref = D.at[z, core, part_e(row)]
        return rc(ref, ref, row_s.at[z, v], row_r.at[z, row], row_dev(v))

    def along_from(z, v):
        r = lax.rem(row + v, Y)
        ref = D.at[z, core, part_e(r)]
        return rc(ref, ref, row_s.at[z, v], row_r.at[z, r], row_dev(v))

    def hand(z):
        ref = D.at[z, core]
        return rc(ref, ref, sib_s.at[8 + z], sib_r.at[8 + z], me_sib)

    def handed(z):
        ref = D.at[z, 1 - core]
        return rc(ref, ref, sib_s.at[8 + z], sib_r.at[8 + z], me_sib)

    def turn(i):
        return slot((i + 1) // 2 * (2 * lax.rem(i, 2) - 1))

    def forward(z):
        far_from(z).wait_recv()
        for v in range(1, Y):
            along(z, v).start()

    def ready(i):
        z = turn(i)
        for v in range(1, Y):
            along_from(z, v).wait_recv()
        hand(z).start()

    pl.when(first)(encode_first)
    pl.when(second)(fetch)
    prepare()
    near = [0] + [w for o in range(1, H + 1) for w in (o, Z - o)][: Z - 1]

    @pl.when(second)
    def _():
        encode_second()
        for o in near:
            if o:
                far(o).start()
            far(Z + o).start()
        hand(blk).start()
        handed(blk).wait_recv()
        run(blk, s1, None, None)

    @pl.when(first)
    def _():
        forward(blk)

    @pl.loop(1, Z)
    def _(i):
        forward(turn(i))

    @pl.when(first)
    def _():
        ready(0)
        handed(blk).wait_recv()
        run(blk, s1, None, None)

    ready(1)

    @pl.loop(0, H - 1)
    def _(g):
        for v in range(2):
            i = 2 * g + 1 + v
            ready(i + 1)
            handed(turn(i)).wait_recv()
            run(turn(i), (s0, s1)[v], turn(i - 1), (s1, s0)[v])

    handed(turn(Z - 1)).wait_recv()
    run(turn(Z - 1), s0, turn(Z - 2), s1)
    run(None, None, turn(Z - 1), s0)

    wide = acc.shape[0] * SUB
    flat = jnp.max(acc[...].reshape(wide, T).T, axis=0, keepdims=True)
    lane = iota((2 * Z, wide), 1)
    apart = jnp.where(lane // (2 * SUB) == iota((2 * Z, wide), 0), flat, 0.0)
    lane = iota((wide, 2 * SUB), 0)
    tile = lane % SUB * 2 + lane // SUB % 2
    pick = (tile == iota((wide, 2 * SUB), 1)).astype(F32)
    out_ref[...] = jnp.dot(
        apart, pick, preferred_element_type=F32, precision=lax.Precision.HIGHEST
    )

    @pl.when(first)
    def _():
        c_conv.wait_send()
        c_mix.wait_send()
        c_q.wait_send()
        for l in range(2):
            for o in range(1, G):
                part = U.at[l, chip_rows(chip)]
                rc(part, part, gat_s.at[l, o], gat_r.at[l, chip], chip_dev(peer(o))).wait_send()
        for c in range(G):
            hop(c).wait_send()
        for v in range(1, Y):
            along(blk, v).wait_send()

    @pl.when(second)
    def _():
        c_own.wait_send()
        c_wp.wait_send()
        c_conv_all.wait_send()
        c_mix_all(0).wait_send()
        c_mix_all(1).wait_send()
        for kind in range(4):
            for o in range(1, G):
                push(kind, o, chip).wait_send()
        for o in range(1, 2 * Z):
            far(o).wait_send()

    for i in range(Z):
        hand(i).wait_send()
    for i in range(1, Z):
        for v in range(1, Y):
            along(slot(i), v).wait_send()


def solution(mesh):
    G = mesh.shape["bank"] // 2
    Z = mesh.shape["blk"]

    def per_device(q, cw, mw, pw, taps, rf, sl):
        half_ch, T = q.shape[1:]
        ch = 2 * half_ch
        C = mw.shape[2]
        E = pw.shape[0]
        F = rf.shape[0]
        LO = F // SUB
        dma = pltpu.SemaphoreType.DMA
        vmem = pl.BlockSpec(memory_space=pltpu.VMEM)
        smem = pl.BlockSpec(memory_space=pltpu.SMEM)
        anyw = pl.BlockSpec(memory_space=pl.ANY)
        cw = jnp.transpose(cw, (0, 1, 3, 2))
        pw = jnp.transpose(pw)
        return pl.pallas_call(
            functools.partial(kernel, G, Z),
            out_shape=jax.ShapeDtypeStruct((2 * Z, 2 * SUB), F32),
            in_specs=[anyw, anyw, anyw, anyw, smem, anyw, smem],
            out_specs=vmem,
            scratch_shapes=[
                pltpu.VMEM(q.shape, BF),
                pltpu.VMEM(cw.shape, BF),
                pltpu.VMEM(pw.shape, BF),
                pltpu.VMEM((2, G, 2, half_ch, T), BF),
                pltpu.VMEM((2, G, ch, 3 * ch), BF),
                pltpu.VMEM((2, G, 2, half_ch, C), BF),
                pltpu.VMEM((E, ch), BF),
                pltpu.VMEM((E, ch), BF),
                pltpu.VMEM((E, C), BF),
                pltpu.VMEM((ch, T), BF),
                pltpu.VMEM((ch, T), BF),
                pltpu.VMEM((G, ch, T), BF),
                pltpu.VMEM((2, C, T), BF),
                pltpu.VMEM((Z, 2, E, T), BF),
                pltpu.VMEM((F, E), BF),
                pltpu.VMEM((E // T, F + 16, T), F32),
                pltpu.VMEM(((LO + 2 * PAD) * SUB, E), BF),
                pltpu.VMEM((TAPS, LO, SUB, T), F32),
                pltpu.VMEM((2, LO + 2 * PAD, SUB, T), F32),
                pltpu.VMEM((2, LO + 2 * PAD, SUB, T), F32),
                pltpu.VMEM((Z * 4, SUB, T), F32),
                dma((5,)),
                dma((8 + Z,)),
                dma((8 + Z,)),
                dma((2, G)),
                dma((2, G)),
                dma((G,)),
                dma((G,)),
                dma((4, G)),
                dma((4, G)),
                dma((2 * Z,)),
                dma((Z,)),
                dma((Z, G // 2)),
                dma((Z, G // 2)),
            ],
            compiler_params=pltpu.CompilerParams(
                collective_id=0,
                has_side_effects=True,
                vmem_limit_bytes=60 * 1024 * 1024,
            ),
        )(q, cw, mw, pw, taps, rf, sl)

    return jax.shard_map(
        per_device,
        mesh=mesh,
        in_specs=(
            P("blk", "bank", None),
            P("phase", None, "bank", None),
            P("phase", "bank", None),
            P(None, "bank"),
            P(),
            P(("phase", "bank", "blk"), None),
            P(("phase", "bank", "blk"), None),
        ),
        out_specs=P(None, ("phase", "bank", "blk")),
        check_vma=False,
    )
```

time: 86.8 us -> 90.5 us (1.043)
  Pallas kernels: 78 us -> 88.6 us
  local copies, waits for them, and re-layouts: 7.84 us -> 1.3 us
    pallas_call x1, Pallas kernels: 78 us -> 88.6 us  [per_device(): pl.pallas_call(functools.partial(kernel, G, Z), out_shape=jax.ShapeDtypeS...]
    unnamed x12 -> x1, local copies, waits for them, and re-layouts: 6.48 us -> 1.3 us
where the time goes in v2:
time: 90.5 us; the launch traced here: 89.9 us
  Pallas kernels  88.6 us (98%)
  local copies, waits for them, and re-layouts  1.3 us (1%)
    pallas_call x1, Pallas kernels, per_device(): pl.pallas_call(functools.partial(kernel, G, Z), out_shape=jax.ShapeDtypeS...  88.6 us

profile of v2, /device:TPU:1, one launch (start us, length us, event | category | flops | bytes accessed | tf_op | source)
XLA Modules:
  0.0 89.9 jit_solution(16394825339344438013)
XLA Ops:
  0.0 88.6 %shard_map.73 = f32[16,16]{1,0:T(8,128)} custom-call(bf16[2,64,128]{2,1,0:T(8,128)(2,1)} %q_hbm.1, bf16[2,3,32,64]{3,2,1,0:T(8,128)(2,1)} %bitcast.3, bf16[2,64,1024]{2,1,0:T(8,128)(2,1)} %mw_ref.1, bf16[64,512]{1,0:T(8,128)(2,1)} %bitcast.2, f32[7]{0:T(128)} %taps_ref.1, bf16[2048,512]{1,0:T(8,128)(2,1)} %rf_ref.1, s32[1,16]{1,0:T(1,128)} %sl_ref.1), custom_call_target="tpu_custom_call" | custom-call | tf_op jit(solution)/shard_map/pallas_call | solution.py:470
  88.6 1.3 %copy.9 = f32[16,16]{1,0:T(8,128)} copy(f32[16,16]{1,0:T(8,128)} %shard_map.73) | data formatting | bytes 2048

commit v3 on v2

--- a/solution.py
+++ b/solution.py
@@ -14,13 +14,14 @@
 PAD = 4
 STEPS = 4
 GROUP = 8
+CHUNKS = 4
 
 
 def kernel(
     G, Z, q_hbm, cw_hbm, mw_ref, pw_hbm, taps_ref, rf_ref, sl_ref, out_ref,
-    q_ref, cw_ref, pw_ref, wraw, wconv, wfull, wown, wsib, wproj, hin, hout, hall, U, D,
+    q_ref, cw_ref, pw_ref, wraw, wconv, wfull, wown, wsib, wproj, hin, hout, hall, h4, U, D,
     rbuf, r32, rperm, wtab, s0, s1, acc,
-    loc, sib_s, sib_r, gat_s, gat_r, hop_s, hop_r, par_s, par_r, far_s, far_r, row_s, row_r,
+    loc, sib_s, sib_r, gat_s, gat_r, hop_s, hop_r, par_s, par_r, ring_s, ring_r, cross_s, cross_r,
 ):
     half_ch = q_ref.shape[1]
     ch = 2 * half_ch
@@ -33,7 +34,6 @@
     LO = F // SUB
     per_step = (LO + 2 * PAD) // STEPS
     out_step = LO // STEPS
-    Y = G // 2
     H = Z // 2
 
     phase = lax.axis_index("phase")
@@ -41,10 +41,8 @@
     blk = lax.axis_index("blk")
     core = lax.rem(bank, 2)
     chip = bank // 2
-    col = chip // Y
-    row = lax.rem(chip, Y)
     me_sib = (phase, chip * 2 + 1 - core, blk)
-    across = lax.rem(chip + Y, G) * 2 + core
+    across = lax.rem(chip + G // 2, G) * 2 + core
     first = phase == 0
     second = phase == 1
 
@@ -54,11 +52,11 @@
     def chip_dev(c):
         return (phase, c * 2 + core, blk)
 
-    def row_dev(v):
-        return (phase, (col * Y + lax.rem(row + v, Y)) * 2 + core, blk)
-
     def slot(shift):
         return lax.rem(blk + Z + shift, Z)
+
+    up = (phase, bank, slot(1))
+    down = (phase, bank, slot(-1))
 
     load_q = pltpu.make_async_copy(q_hbm, q_ref, loc.at[2])
     load_c = pltpu.make_async_copy(cw_hbm, cw_ref, loc.at[3])
@@ -69,8 +67,7 @@
 
     barrier = pltpu.get_barrier_semaphore()
     greet = [me_sib] + [chip_dev(peer(o)) for o in range(1, G)]
-    greet += [(phase, bank, slot(o)) for o in range(1, Z)]
-    greet += [(1 - phase, across, slot(o)) for o in range(1, Z)]
+    greet += [up, down]
     greet += [(1 - phase, c * 2 + core, blk) for c in range(G)]
     for dev in greet:
         pl.semaphore_signal(
@@ -104,11 +101,7 @@
     eh = E // 2
     my_e = pl.ds(pl.multiple_of(core * eh, eh), eh)
     its_e = pl.ds(pl.multiple_of((1 - core) * eh, eh), eh)
-    eq = E // Y
-
-    def part_e(r):
-        return pl.ds(pl.multiple_of(r * eq, eq), eq)
-
+    ec = E // CHUNKS
     load_c.wait()
     for l in range(2):
         flat = None
@@ -130,18 +123,16 @@
     c_wp = rc(wproj.at[my_e], wproj.at[my_e], sib_s.at[4], sib_r.at[4], me_sib)
     c_conv_all = rc(wraw.at[:, :, core], wraw.at[:, :, core], sib_s.at[5], sib_r.at[5], me_sib)
 
-    def c_mix_all(l):
-        return rc(
-            wfull.at[l, :, core], wfull.at[l, :, core], sib_s.at[6 + l], sib_r.at[6 + l], me_sib
-        )
+    c_mix_all = rc(wfull.at[0, :, core], wfull.at[0, :, core], sib_s.at[6], sib_r.at[6], me_sib)
+    c_mix_one = rc(mw_ref.at[1], wfull.at[1, chip, core], sib_s.at[7], sib_r.at[7], me_sib)
 
     def push(kind, o, c):
         if kind == 0:
             src = dst = wraw.at[:, c, core]
-        elif kind == 3:
+        elif kind == 2:
             src = dst = wproj.at[my_e, chip_rows(c)]
         else:
-            src, dst = mw_ref.at[kind - 1], wfull.at[kind - 1, c, core]
+            src, dst = mw_ref.at[0], wfull.at[0, c, core]
         return rc(src, dst, par_s.at[kind, o], par_r.at[kind, c], chip_dev(peer(o)))
 
     spread = ones(
@@ -199,9 +190,10 @@
         return rc(hout, hall.at[chip], hop_s.at[c], hop_r.at[chip], (1, c * 2 + core, blk))
 
     def fetch():
-        for kind in range(3):
+        for kind in range(2):
             for o in range(1, G):
                 push(kind, o, chip).start()
+        c_mix_one.start()
         load_p.wait()
         move = ones(iota((half_ch, ch), 1) == iota((half_ch, ch), 0) + core * half_ch)
         wown[...] = turned(pw_ref[...], move).astype(BF)
@@ -209,14 +201,18 @@
         c_own.wait_recv()
         wproj[my_e, chip_rows(chip)] = wown[my_e] + wsib[my_e]
         for o in range(1, G):
-            push(3, o, chip).start()
+            push(2, o, chip).start()
+
+    def share4(o, c):
+        part = h4.at[chip_rows(c)]
+        return rc(part, part, gat_s.at[0, o], gat_r.at[0, c], chip_dev(peer(o)))
 
     def encode_second():
         load_m.wait()
-        for kind in range(4):
+        for kind, onward in enumerate((c_conv_all, c_mix_all, c_wp)):
             for o in range(1, G):
                 push(kind, o, peer(o)).wait_recv()
-            (c_conv_all, c_mix_all(0), c_mix_all(1), c_wp)[kind].start()
+            onward.start()
         c_conv_all.wait_recv()
         for l in range(2):
             for c in range(G):
@@ -230,10 +226,19 @@
                 x = jnp.concatenate([v[c * ch : (c + 1) * ch] for v in sides], axis=0)
                 a = jnp.dot(wconv[l, c], x, preferred_element_type=F32)
                 U[l, c * ch : (c + 1) * ch] = jax.nn.gelu(a, approximate=True).astype(BF)
-            c_mix_all(l).wait_recv()
-            h = mixed(h, wfull[l].reshape(C, C), U[l]).astype(F32)
+            if l == 0:
+                c_mix_all.wait_recv()
+                hall[...] = mixed(h, wfull[0].reshape(C, C), U[0]).reshape(G, ch, T)
+                h = hall[...].reshape(C, T).astype(F32)
+        c_mix_one.wait_recv()
+        last = mixed(hall[chip].astype(F32), wfull[1, chip].reshape(ch, C), U[1])
+        h4[chip_rows(chip)] = last
+        for o in range(1, G):
+            share4(o, chip).start()
         c_wp.wait_recv()
-        p = jnp.dot(wproj[...], h.astype(BF), preferred_element_type=F32)
+        for o in range(1, G):
+            share4(o, peer(o)).wait_recv()
+        p = jnp.dot(wproj[...], h4[...], preferred_element_type=F32)
         norm = lax.rsqrt(jnp.sum(p * p, axis=0, keepdims=True) / E + 1e-6)
         D[blk, core] = (p * norm).astype(BF)
 
@@ -321,23 +326,22 @@
             if new is not None:
                 multiply(new, c, into)
 
-    def far(o):
-        ref = D.at[blk, core, part_e(row)]
-        dev = (phase, bank, slot(o)) if o < Z else (1 - phase, across, slot(o - Z))
-        return rc(ref, ref, far_s.at[o], far_r.at[blk], dev)
-
-    def far_from(z):
-        ref = D.at[z, core, part_e(row)]
-        return rc(ref, ref, far_s.at[0], far_r.at[z], me_sib)
-
-    def along(z, v):
-        ref = D.at[z, core, part_e(row)]
-        return rc(ref, ref, row_s.at[z, v], row_r.at[z, row], row_dev(v))
-
-    def along_from(z, v):
-        r = lax.rem(row + v, Y)
-        ref = D.at[z, core, part_e(r)]
-        return rc(ref, ref, row_s.at[z, v], row_r.at[z, r], row_dev(v))
+    def bit(z, k):
+        return D.at[z, core, pl.ds(pl.multiple_of(k * ec, ec), ec)]
+
+    def cross(k):
+        ref = bit(blk, k)
+        return rc(ref, ref, cross_s.at[k], cross_r.at[k], (1 - phase, across, blk))
+
+    def ring(way, step, k):
+        ref = bit(slot((1 - way * 2) * (1 - step)), k)
+        sems = ring_s.at[way, step, k], ring_r.at[way, step, k]
+        return rc(ref, ref, *sems, (up, down)[way])
+
+    def arrival(way, step, k):
+        ref = bit(slot((way * 2 - 1) * step), k)
+        sems = ring_s.at[way, step, k], ring_r.at[way, step, k]
+        return rc(ref, ref, *sems, (up, down)[way])
 
     def hand(z):
         ref = D.at[z, core]
@@ -347,63 +351,67 @@
         ref = D.at[z, 1 - core]
         return rc(ref, ref, sib_s.at[8 + z], sib_r.at[8 + z], me_sib)
 
-    def turn(i):
-        return slot((i + 1) // 2 * (2 * lax.rem(i, 2) - 1))
-
-    def forward(z):
-        far_from(z).wait_recv()
-        for v in range(1, Y):
-            along(z, v).start()
-
-    def ready(i):
-        z = turn(i)
-        for v in range(1, Y):
-            along_from(z, v).wait_recv()
-        hand(z).start()
+    def order(i):
+        return slot((i + 1) // 2 * (1 - 2 * lax.rem(i, 2)))
+
+    half = CHUNKS // 2
 
     pl.when(first)(encode_first)
     pl.when(second)(fetch)
     prepare()
-    near = [0] + [w for o in range(1, H + 1) for w in (o, Z - o)][: Z - 1]
 
     @pl.when(second)
     def _():
         encode_second()
-        for o in near:
-            if o:
-                far(o).start()
-            far(Z + o).start()
-        hand(blk).start()
-        handed(blk).wait_recv()
-        run(blk, s1, None, None)
-
-    @pl.when(first)
-    def _():
-        forward(blk)
-
-    @pl.loop(1, Z)
-    def _(i):
-        forward(turn(i))
-
-    @pl.when(first)
-    def _():
-        ready(0)
-        handed(blk).wait_recv()
-        run(blk, s1, None, None)
-
-    ready(1)
-
-    @pl.loop(0, H - 1)
-    def _(g):
-        for v in range(2):
-            i = 2 * g + 1 + v
-            ready(i + 1)
-            handed(turn(i)).wait_recv()
-            run(turn(i), (s0, s1)[v], turn(i - 1), (s1, s0)[v])
-
-    handed(turn(Z - 1)).wait_recv()
-    run(turn(Z - 1), s0, turn(Z - 2), s1)
-    run(None, None, turn(Z - 1), s0)
+        for k in range(CHUNKS):
+            cross(k).start()
+
+    for k in range(CHUNKS):
+        @pl.when(first)
+        def _():
+            cross(k).wait_recv()
+
+        for way in range(2):
+            ring(way, 1, k).start()
+    hand(blk).start()
+
+    @pl.loop(1, H)
+    def _(step):
+        for k in range(CHUNKS):
+            for way in range(2):
+                arrival(way, step, k).wait_recv()
+
+                @pl.when((step < H - 1) | (k // half == way))
+                def _():
+                    ring(way, step + 1, k).start()
+
+        for way in range(2):
+            hand(slot((way * 2 - 1) * step)).start()
+
+        @pl.when(step == 1)
+        def _():
+            handed(blk).wait_recv()
+            run(blk, s1, None, None)
+
+        @pl.when(step > 1)
+        def _():
+            for v in range(2):
+                i = 2 * step - 3 + v
+                handed(order(i)).wait_recv()
+                run(order(i), (s0, s1)[v], order(i - 1), (s1, s0)[v])
+
+    far = order(Z - 1)
+    for v in range(2):
+        i = Z - 3 + v
+        handed(order(i)).wait_recv()
+        run(order(i), (s0, s1)[v], order(i - 1), (s1, s0)[v])
+        if v == 0:
+            for k in range(CHUNKS):
+                arrival(k // half, H, k).wait_recv()
+            hand(far).start()
+    handed(far).wait_recv()
+    run(far, s0, order(Z - 2), s1)
+    run(None, None, far, s0)
 
     wide = acc.shape[0] * SUB
     flat = jnp.max(acc[...].reshape(wide, T).T, axis=0, keepdims=True)
@@ -427,27 +435,29 @@
                 rc(part, part, gat_s.at[l, o], gat_r.at[l, chip], chip_dev(peer(o))).wait_send()
         for c in range(G):
             hop(c).wait_send()
-        for v in range(1, Y):
-            along(blk, v).wait_send()
 
     @pl.when(second)
     def _():
         c_own.wait_send()
         c_wp.wait_send()
         c_conv_all.wait_send()
-        c_mix_all(0).wait_send()
-        c_mix_all(1).wait_send()
-        for kind in range(4):
+        c_mix_all.wait_send()
+        c_mix_one.wait_send()
+        for kind in range(3):
             for o in range(1, G):
                 push(kind, o, chip).wait_send()
-        for o in range(1, 2 * Z):
-            far(o).wait_send()
+        for o in range(1, G):
+            share4(o, chip).wait_send()
+        for k in range(CHUNKS):
+            cross(k).wait_send()
 
     for i in range(Z):
         hand(i).wait_send()
-    for i in range(1, Z):
-        for v in range(1, Y):
-            along(slot(i), v).wait_send()
+    for k in range(CHUNKS):
+        for way in range(2):
+            for step in range(1, H):
+                ring(way, step, k).wait_send()
+        ring(k // half, H, k).wait_send()
 
 
 def solution(mesh):
@@ -485,6 +495,7 @@
                 pltpu.VMEM((ch, T), BF),
                 pltpu.VMEM((ch, T), BF),
                 pltpu.VMEM((G, ch, T), BF),
+                pltpu.VMEM((C, T), BF),
                 pltpu.VMEM((2, C, T), BF),
                 pltpu.VMEM((Z, 2, E, T), BF),
                 pltpu.VMEM((F, E), BF),
@@ -501,12 +512,12 @@
                 dma((2, G)),
                 dma((G,)),
                 dma((G,)),
-                dma((4, G)),
-                dma((4, G)),
-                dma((2 * Z,)),
-                dma((Z,)),
-                dma((Z, G // 2)),
-                dma((Z, G // 2)),
+                dma((3, G)),
+                dma((3, G)),
+                dma((2, Z // 2 + 1, CHUNKS)),
+                dma((2, Z // 2 + 1, CHUNKS)),
+                dma((CHUNKS,)),
+                dma((CHUNKS,)),
             ],
             compiler_params=pltpu.CompilerParams(
                 collective_id=0,

time: 90.5 us -> 77.5 us (0.86)
  Pallas kernels: 88.6 us -> 76 us
    pallas_call x1, Pallas kernels: 88.6 us -> 76 us  [per_device(): pl.pallas_call(functools.partial(kernel, G, Z), out_shape=jax.ShapeDtypeS...]
where the time goes in v3:
time: 77.5 us; the launch traced here: 77.3 us
  Pallas kernels  76 us (98%)
  local copies, waits for them, and re-layouts  1.3 us (2%)
    pallas_call x1, Pallas kernels, per_device(): pl.pallas_call(functools.partial(kernel, G, Z), out_shape=jax.ShapeDtypeS...  76 us

profile of v3, /device:TPU:1, one launch (start us, length us, event | category | flops | bytes accessed | tf_op | source)
XLA Modules:
  0.0 77.3 jit_solution(11476543296005141046)
XLA Ops:
  0.0 76.0 %shard_map.73 = f32[16,16]{1,0:T(8,128)} custom-call(bf16[2,64,128]{2,1,0:T(8,128)(2,1)} %q_hbm.1, bf16[2,3,32,64]{3,2,1,0:T(8,128)(2,1)} %bitcast.3, bf16[2,64,1024]{2,1,0:T(8,128)(2,1)} %mw_ref.1, bf16[64,512]{1,0:T(8,128)(2,1)} %bitcast.2, f32[7]{0:T(128)} %taps_ref.1, bf16[2048,512]{1,0:T(8,128)(2,1)} %rf_ref.1, s32[1,16]{1,0:T(1,128)} %sl_ref.1), custom_call_target="tpu_custom_call" | custom-call | tf_op jit(solution)/shard_map/pallas_call | solution.py:480
  76.0 1.3 %copy.9 = f32[16,16]{1,0:T(8,128)} copy(f32[16,16]{1,0:T(8,128)} %shard_map.73) | data formatting | bytes 2048

commit v4 on v3

--- a/solution.py
+++ b/solution.py
@@ -10,10 +10,10 @@
 BF = jnp.bfloat16
 F32 = jnp.float32
 TAPS = 7
+MID = TAPS // 2
 SUB = 8
 PAD = 4
-STEPS = 4
-GROUP = 8
+GROUP = 4
 CHUNKS = 4
 
 
@@ -32,8 +32,6 @@
     slices = sl_ref.shape[1]
     gw = cw_ref.shape[2]
     LO = F // SUB
-    per_step = (LO + 2 * PAD) // STEPS
-    out_step = LO // STEPS
     H = Z // 2
 
     phase = lax.axis_index("phase")
@@ -200,8 +198,6 @@
         c_own.start()
         c_own.wait_recv()
         wproj[my_e, chip_rows(chip)] = wown[my_e] + wsib[my_e]
-        for o in range(1, G):
-            push(2, o, chip).start()
 
     def share4(o, c):
         part = h4.at[chip_rows(c)]
@@ -209,10 +205,12 @@
 
     def encode_second():
         load_m.wait()
-        for kind, onward in enumerate((c_conv_all, c_mix_all, c_wp)):
+        for kind, onward in enumerate((c_conv_all, c_mix_all)):
             for o in range(1, G):
                 push(kind, o, peer(o)).wait_recv()
             onward.start()
+        for o in range(1, G):
+            push(2, o, chip).start()
         c_conv_all.wait_recv()
         for l in range(2):
             for c in range(G):
@@ -235,9 +233,12 @@
         h4[chip_rows(chip)] = last
         for o in range(1, G):
             share4(o, chip).start()
-        c_wp.wait_recv()
+        for o in range(1, G):
+            push(2, o, peer(o)).wait_recv()
+        c_wp.start()
         for o in range(1, G):
             share4(o, peer(o)).wait_recv()
+        c_wp.wait_recv()
         p = jnp.dot(wproj[...], h4[...], preferred_element_type=F32)
         norm = lax.rsqrt(jnp.sum(p * p, axis=0, keepdims=True) / E + 1e-6)
         D[blk, core] = (p * norm).astype(BF)
@@ -271,7 +272,6 @@
         for k in range(slices):
             total = total + sl_ref[0, k]
             ends.append(total)
-        scale = E ** (-0.5)
 
         @pl.loop(0, LO // 8)
         def _(i):
@@ -286,45 +286,40 @@
             t = (lax.broadcasted_iota(jnp.int32, shape, 2) + lo) & (T - 1)
             at = pl.ds(i * 8, 8)
             for k in range(TAPS):
-                j = k - TAPS // 2
-                inside = jnp.where((r + j >= begin) & (r + j < end), taps_ref[k] * scale, 0.0)
+                j = k - MID
+                if j == 0:
+                    continue
+                inside = jnp.where((r + j >= begin) & (r + j < end), taps_ref[k] / taps_ref[MID], 0.0)
                 wtab[k, at] = jnp.where((t + j >= 0) & (t + j < T), inside, 0.0)
 
-        acc[...] = jnp.full(acc.shape, -jnp.inf, F32)
-
-    def multiply(z, c, into):
+    def multiply(z, into):
         both = jnp.concatenate([D[z, 0], D[z, 1]], axis=1)
-        rows = pl.ds(pl.multiple_of(c * (per_step * SUB), 16), per_step * SUB)
-        s = jnp.dot(rperm[rows], both, preferred_element_type=F32)
-        for i in range(per_step):
-            turn = lax.rem(2 * LO + PAD - c * per_step - i, T)
+        s = jnp.dot(rperm[...], both, preferred_element_type=F32)
+        for i in range(LO + 2 * PAD):
             for n in range(2):
                 piece = s[i * SUB : (i + 1) * SUB, n * T : (n + 1) * T]
-                into[n, c * per_step + i] = pltpu.roll(piece, turn, 1)
-
-    def select(z, c, s):
-        best = [None, None]
-        for g in range(out_step // GROUP):
-            lo = c * out_step + g * GROUP
-            w = [wtab[k, pl.ds(lo, GROUP)] for k in range(TAPS)]
+                into[n, i] = pltpu.roll(piece, (2 * LO + PAD - i) % T, 1)
+
+    def select(z, s):
+        for side in range(2):
+            best = [None, None]
+            for lo in range(side * LO // 2, (side + 1) * LO // 2, GROUP):
+                w = [None if k == MID else wtab[k, lo : lo + GROUP] for k in range(TAPS)]
+                for n in range(2):
+                    win = s[n, lo + PAD - MID : lo + PAD + MID + GROUP]
+                    t = [win[k : k + GROUP] for k in range(TAPS)]
+                    t = [v if k == MID else w[k] * v for k, v in enumerate(t)]
+                    f = (t[0] + t[1]) + (t[2] + t[3]) + (t[4] + t[5] + t[6])
+                    f = jnp.max(f, axis=0)
+                    best[n] = f if best[n] is None else jnp.maximum(best[n], f)
             for n in range(2):
-                win = s[n, pl.ds(lo + PAD - 3, GROUP + 6)]
-                f = w[0] * win[0:GROUP]
-                for k in range(1, TAPS):
-                    f = f + w[k] * win[k : k + GROUP]
-                f = jnp.max(f, axis=0)
-                best[n] = f if best[n] is None else jnp.maximum(best[n], f)
-        for n in range(2):
-            at = (z * 2 + n) * 2 + c // (STEPS // 2)
-            acc[at] = jnp.maximum(acc[at], best[n])
+                acc[(z * 2 + n) * 2 + side] = best[n]
 
     def run(new, into, old, held):
-        @pl.loop(0, STEPS)
-        def _(c):
-            if old is not None:
-                select(old, c, held)
-            if new is not None:
-                multiply(new, c, into)
+        if old is not None:
+            select(old, held)
+        if new is not None:
+            multiply(new, into)
 
     def bit(z, k):
         return D.at[z, core, pl.ds(pl.multiple_of(k * ec, ec), ec)]
@@ -355,6 +350,7 @@
         return slot((i + 1) // 2 * (1 - 2 * lax.rem(i, 2)))
 
     half = CHUNKS // 2
+    far = order(Z - 1)
 
     pl.when(first)(encode_first)
     pl.when(second)(fetch)
@@ -375,46 +371,56 @@
             ring(way, 1, k).start()
     hand(blk).start()
 
-    @pl.loop(1, H)
-    def _(step):
-        for k in range(CHUNKS):
-            for way in range(2):
-                arrival(way, step, k).wait_recv()
-
-                @pl.when((step < H - 1) | (k // half == way))
-                def _():
-                    ring(way, step + 1, k).start()
-
+    handed(blk).wait_recv()
+    run(blk, s1, None, None)
+
+    def relay(step, k):
+        for way in range(2):
+            arrival(way, step, k).wait_recv()
+
+            @pl.when((step < H - 1) | (k // half == way))
+            def _():
+                ring(way, step + 1, k).start()
+
+    def hand_both(step):
         for way in range(2):
             hand(slot((way * 2 - 1) * step)).start()
 
-        @pl.when(step == 1)
+    for k in range(CHUNKS):
+        relay(1, k)
+    hand_both(1)
+
+    @pl.loop(2, H + 1)
+    def _(step):
+        for v in range(2):
+            i = 2 * step - 3 + v
+
+            @pl.when(step < H)
+            def _():
+                for k in range(half):
+                    relay(step, v * half + k)
+
+            handed(order(i)).wait_recv()
+            run(order(i), (s0, s1)[v], order(i - 1), (s1, s0)[v])
+
+            if v == 0:
+                @pl.when(step == H)
+                def _():
+                    for k in range(CHUNKS):
+                        arrival(k // half, H, k).wait_recv()
+                    hand(far).start()
+
+        @pl.when(step < H)
         def _():
-            handed(blk).wait_recv()
-            run(blk, s1, None, None)
-
-        @pl.when(step > 1)
-        def _():
-            for v in range(2):
-                i = 2 * step - 3 + v
-                handed(order(i)).wait_recv()
-                run(order(i), (s0, s1)[v], order(i - 1), (s1, s0)[v])
-
-    far = order(Z - 1)
-    for v in range(2):
-        i = Z - 3 + v
-        handed(order(i)).wait_recv()
-        run(order(i), (s0, s1)[v], order(i - 1), (s1, s0)[v])
-        if v == 0:
-            for k in range(CHUNKS):
-                arrival(k // half, H, k).wait_recv()
-            hand(far).start()
+            hand_both(step)
+
     handed(far).wait_recv()
     run(far, s0, order(Z - 2), s1)
     run(None, None, far, s0)
 
     wide = acc.shape[0] * SUB
     flat = jnp.max(acc[...].reshape(wide, T).T, axis=0, keepdims=True)
+    flat = flat * (taps_ref[MID] * E ** (-0.5))
     lane = iota((2 * Z, wide), 1)
     apart = jnp.where(lane // (2 * SUB) == iota((2 * Z, wide), 0), flat, 0.0)
     lane = iota((wide, 2 * SUB), 0)

time: 77.5 us -> 71.9 us (0.928)
  Pallas kernels: 76 us -> 70.4 us
    pallas_call x1, Pallas kernels: 76 us -> 70.4 us  [per_device(): pl.pallas_call(functools.partial(kernel, G, Z), out_shape=jax.ShapeDtypeS...]
where the time goes in v4:
time: 71.9 us; the launch traced here: 71.7 us
  Pallas kernels  70.4 us (98%)
  local copies, waits for them, and re-layouts  1.3 us (2%)
    pallas_call x1, Pallas kernels, per_device(): pl.pallas_call(functools.partial(kernel, G, Z), out_shape=jax.ShapeDtypeS...  70.4 us

profile of v4, /device:TPU:1, one launch (start us, length us, event | category | flops | bytes accessed | tf_op | source)
XLA Modules:
  0.0 71.7 jit_solution(16633195588695077398)
XLA Ops:
  0.0 70.4 %shard_map.73 = f32[16,16]{1,0:T(8,128)} custom-call(bf16[2,64,128]{2,1,0:T(8,128)(2,1)} %q_hbm.1, bf16[2,3,32,64]{3,2,1,0:T(8,128)(2,1)} %bitcast.3, bf16[2,64,1024]{2,1,0:T(8,128)(2,1)} %mw_ref.1, bf16[64,512]{1,0:T(8,128)(2,1)} %bitcast.2, f32[7]{0:T(128)} %taps_ref.1, bf16[2048,512]{1,0:T(8,128)(2,1)} %rf_ref.1, s32[1,16]{1,0:T(1,128)} %sl_ref.1), custom_call_target="tpu_custom_call" | custom-call | tf_op jit(solution)/shard_map/pallas_call | solution.py:486
  70.4 1.3 %copy.9 = f32[16,16]{1,0:T(8,128)} copy(f32[16,16]{1,0:T(8,128)} %shard_map.73) | data formatting | bytes 2048

commit v5 on v4

--- a/solution.py
+++ b/solution.py
@@ -14,7 +14,7 @@
 SUB = 8
 PAD = 4
 GROUP = 4
-CHUNKS = 4
+CHUNKS = 2
 
 
 def kernel(
@@ -163,8 +163,8 @@
         c_q.wait_recv()
         c_conv.wait_recv()
         h = hin[...].astype(F32)
+        wide = expand(wraw[0, chip])
         for l in range(2):
-            wide = expand(wraw[l, chip])
             x = jnp.concatenate(shifts(h, 1 << l), axis=0)
             a = jnp.dot(wide, x, preferred_element_type=F32)
             part = U.at[l, chip_rows(chip)]
@@ -172,6 +172,7 @@
             for o in range(1, G):
                 rc(part, part, gat_s.at[l, o], gat_r.at[l, chip], chip_dev(peer(o))).start()
             if l == 0:
+                wide = expand(wraw[1, chip])
                 load_m.wait()
                 c_mix.wait_recv()
             for o in range(1, G):
@@ -392,14 +393,14 @@
 
     @pl.loop(2, H + 1)
     def _(step):
+        @pl.when(step < H)
+        def _():
+            for k in range(CHUNKS):
+                relay(step, k)
+            hand_both(step)
+
         for v in range(2):
             i = 2 * step - 3 + v
-
-            @pl.when(step < H)
-            def _():
-                for k in range(half):
-                    relay(step, v * half + k)
-
             handed(order(i)).wait_recv()
             run(order(i), (s0, s1)[v], order(i - 1), (s1, s0)[v])
 
@@ -409,10 +410,6 @@
                     for k in range(CHUNKS):
                         arrival(k // half, H, k).wait_recv()
                     hand(far).start()
-
-        @pl.when(step < H)
-        def _():
-            hand_both(step)
 
     handed(far).wait_recv()
     run(far, s0, order(Z - 2), s1)

time: 71.9 us -> 70.3 us (0.978)
  Pallas kernels: 70.4 us -> 68.8 us
    pallas_call x1, Pallas kernels: 70.4 us -> 68.8 us  [per_device(): pl.pallas_call(functools.partial(kernel, G, Z), out_shape=jax.ShapeDtypeS...]
where the time goes in v5:
time: 70.3 us; the launch traced here: 70.1 us
  Pallas kernels  68.8 us (98%)
  local copies, waits for them, and re-layouts  1.3 us (2%)
    pallas_call x1, Pallas kernels, per_device(): pl.pallas_call(functools.partial(kernel, G, Z), out_shape=jax.ShapeDtypeS...  68.8 us

profile of v5, /device:TPU:1, one launch (start us, length us, event | category | flops | bytes accessed | tf_op | source)
XLA Modules:
  0.0 70.1 jit_solution(4333656038068142627)
XLA Ops:
  0.0 68.8 %shard_map.73 = f32[16,16]{1,0:T(8,128)} custom-call(bf16[2,64,128]{2,1,0:T(8,128)(2,1)} %q_hbm.1, bf16[2,3,32,64]{3,2,1,0:T(8,128)(2,1)} %bitcast.3, bf16[2,64,1024]{2,1,0:T(8,128)(2,1)} %mw_ref.1, bf16[64,512]{1,0:T(8,128)(2,1)} %bitcast.2, f32[7]{0:T(128)} %taps_ref.1, bf16[2048,512]{1,0:T(8,128)(2,1)} %rf_ref.1, s32[1,16]{1,0:T(1,128)} %sl_ref.1), custom_call_target="tpu_custom_call" | custom-call | tf_op jit(solution)/shard_map/pallas_call | solution.py:483
  68.9 1.3 %copy.9 = f32[16,16]{1,0:T(8,128)} copy(f32[16,16]{1,0:T(8,128)} %shard_map.73) | data formatting | bytes 2048

commit v6 on v5

--- a/solution.py
+++ b/solution.py
@@ -158,12 +158,12 @@
     def encode_first():
         c_q.start()
         c_conv.start()
+        hin[mine] = q_ref[core]
+        c_conv.wait_recv()
+        wide = expand(wraw[0, chip])
+        c_q.wait_recv()
         c_mix.start()
-        hin[mine] = q_ref[core]
-        c_q.wait_recv()
-        c_conv.wait_recv()
         h = hin[...].astype(F32)
-        wide = expand(wraw[0, chip])
         for l in range(2):
             x = jnp.concatenate(shifts(h, 1 << l), axis=0)
             a = jnp.dot(wide, x, preferred_element_type=F32)

time: 70.3 us -> 70.4 us (level)
  no operation moved by 1% of the time
where the time goes in v6:
time: 70.4 us; the launch traced here: 70.3 us
  Pallas kernels  69 us (98%)
  local copies, waits for them, and re-layouts  1.3 us (2%)
    pallas_call x1, Pallas kernels, per_device(): pl.pallas_call(functools.partial(kernel, G, Z), out_shape=jax.ShapeDtypeS...  69 us

profile of v6, /device:TPU:1, one launch (start us, length us, event | category | flops | bytes accessed | tf_op | source)
XLA Modules:
  0.0 70.3 jit_solution(70661050232606064)
XLA Ops:
  0.0 69.0 %shard_map.73 = f32[16,16]{1,0:T(8,128)} custom-call(bf16[2,64,128]{2,1,0:T(8,128)(2,1)} %q_hbm.1, bf16[2,3,32,64]{3,2,1,0:T(8,128)(2,1)} %bitcast.3, bf16[2,64,1024]{2,1,0:T(8,128)(2,1)} %mw_ref.1, bf16[64,512]{1,0:T(8,128)(2,1)} %bitcast.2, f32[7]{0:T(128)} %taps_ref.1, bf16[2048,512]{1,0:T(8,128)(2,1)} %rf_ref.1, s32[1,16]{1,0:T(1,128)} %sl_ref.1), custom_call_target="tpu_custom_call" | custom-call | tf_op jit(solution)/shard_map/pallas_call | solution.py:483
  69.0 1.3 %copy.9 = f32[16,16]{1,0:T(8,128)} copy(f32[16,16]{1,0:T(8,128)} %shard_map.73) | data formatting | bytes 2048
